TPU v7x, 512 devices: a whole 4x4x16 slice. The times are simulated.
512 devices in a mesh: row: 32 (over y, z_hi, core), col: 16 (over x, z_lo).
Axes of the slice: x: 4, y: 4, z: 16 (z_hi: 4, z_lo: 4; z = z_hi * 4 + z_lo), core: 2. Of those that a mesh axis runs over, the one named last changes fastest.
Arguments:
- features: bfloat16 [65536, 256], P(('col', 'row')), may hold values from -6 to 6
- grad_out: bfloat16 [65536, 256], P(('row', 'col')), may hold values from -6 to 6
- weight: bfloat16 [256, 256], replicated, may hold values from -0.375 to 0.375
- tiles: bfloat16 [32, 16, 96, 128, 128], P('row', 'col')
- coords: int32 [32, 16, 96, 2], P('row', 'col'), may hold values from 0 to 31, as said below
Outputs:
- grad_features: bfloat16 [65536, 256], P(('col', 'row'))
- grad_weight: float32 [256, 256], replicated
Inputs may be any that keep to these rules, and one draw needn't show every extreme that they name: `coords`: the 96 (tile row, tile column) pairs of one device are distinct; tile rows lie below 16, tile columns below 32.
All inputs are finite; a program needn't handle non-finite values.
Results may differ from a plain program's by a relative error of at most 0.029.
Values may be sent and summed in bfloat16 or wider, within the bound.
No kernel may reach another device: no remote copies, remote signals or barrier semaphores. Data moves between devices by JAX's collectives and lax.ppermute only.
A program may use at most 64 MiB of HBM per device.

v0:
```python
import math

import jax
import jax.numpy as jnp
from jax import lax
from jax.sharding import PartitionSpec as P


def silu_slope(value):
    sig = jax.nn.sigmoid(value)
    return sig * (1.0 + value * (1.0 - sig))


def tile_sum(tile_set, coord_set, source, n_dst, backward):
    width = source.shape[1]
    tile = tile_set.shape[-1]
    blocks = source.reshape(-1, tile, width)
    count = tile_set.shape[0]
    group = max((g for g in range(1, min(32, count) + 1) if count % g == 0))
    tile_groups = tile_set.reshape(count // group, group, tile, tile)
    coord_groups = coord_set.reshape(count // group, group, 2)
    form = "kji,kjh->kih" if backward else "kij,kjh->kih"

    def step(total, item):
        tile_part, coord_part = item
        src_index = coord_part[:, 0] if backward else coord_part[:, 1]
        dst_index = coord_part[:, 1] if backward else coord_part[:, 0]
        picked = jnp.take(blocks, src_index, axis=0)
        product = jnp.einsum(form, tile_part, picked, preferred_element_type=jnp.float32)
        return (total.at[dst_index].add(product), None)

    total, _ = lax.scan(
        step, jnp.zeros((n_dst, tile, width), jnp.float32), (tile_groups, coord_groups)
    )
    return total.reshape(-1, width).astype(jnp.bfloat16)


def on_device(features, grad_out, weight, tiles, coords):
    tile_set = tiles[0, 0]
    coord_set = coords[0, 0]
    local_nodes = features.shape[0]
    tile = tile_set.shape[-1]
    row_tiles = local_nodes * lax.axis_size("col") // tile
    col_tiles = local_nodes * lax.axis_size("row") // tile
    nodes = local_nodes * lax.axis_size("col") * lax.axis_size("row")
    sources = lax.all_gather(features, "row", axis=0, tiled=True)
    partial_value = tile_sum(tile_set, coord_set, sources, row_tiles, False)
    aggregated = (
        lax.psum_scatter(partial_value, "col", scatter_dimension=0, tiled=True)
        .astype(jnp.float32)
        .astype(jnp.bfloat16)
    )
    pre = jnp.dot(aggregated, weight, preferred_element_type=jnp.float32)
    slope_grad = (grad_out.astype(jnp.float32) * silu_slope(pre)).astype(jnp.bfloat16)
    weight_term = jnp.einsum(
        "nh,ng->hg", aggregated, slope_grad, preferred_element_type=jnp.float32
    )
    own_grad = jnp.dot(slope_grad, weight.T, preferred_element_type=jnp.float32).astype(
        jnp.bfloat16
    )
    node_grad = lax.all_gather(own_grad, "col", axis=0, tiled=True)
    back = tile_sum(tile_set, coord_set, node_grad, col_tiles, True)
    grad_features = (
        lax.psum_scatter(back, "row", scatter_dimension=0, tiled=True)
        .astype(jnp.float32)
        .astype(jnp.bfloat16)
    )
    grad_weight = lax.psum(weight_term, ("row", "col")) * (1.0 / math.sqrt(nodes))
    return (grad_features, grad_weight)


def solution(mesh):
    in_specs = (
        P(("col", "row"), None),
        P(("row", "col"), None),
        P(),
        P("row", "col", None, None, None),
        P("row", "col", None, None),
    )
    out_specs = (P(("col", "row"), None), P())
    return jax.shard_map(
        on_device, mesh=mesh, in_specs=in_specs, out_specs=out_specs, check_vma=False
    )
```

profile of v0, /device:TPU:6, one launch (start us, length us, event | category | flops | bytes accessed | tf_op | source)
XLA Modules:
  0.0 904.7 jit_solution(14120223109635473100)
XLA Ops:
  7.2 0.0 copy-start
  7.2 0.0 all-gather.3.cloned.1.call-start
  7.2 0.7 all-gather.3.cloned.1.call-update
  7.9 0.0 reduce-scatter.3.cloned.1.call-start
  8.0 0.8 reshape_squeeze.8
  8.7 85.4 %all-gather.3.cloned.1.call-done = bf16[4096,256]{1,0:T(8,128)(2,1)} async-done(((bf16[128,256]{1,0:T(8,128)(2,1)}), bf16[4096,256]{1,0:T(8,128)(2,1)}) %all-gather.3.cloned.1.call-update) | async-done | bytes 2097168 | tf_op jit(solution)/shard_map/all_gather | solution.py:46
  94.2 0.2 broadcast_in_dim.29
  94.4 44.5 %while.20 = (s32[]{:T(128)}, f32[16,128,256]{2,1,0:T(8,128)S(1)}, s32[3,32,2]{1,2,0:T(2,128)S(1)}, bf16[3,32,128,128]{3,2,1,0:T(8,128)(2,1)}, bf16[32,128,256]{2,1,0:T(8,128)(2,1)}, /*index=5*/s32[]{:T(128)}) while((s32[]{:T(128)}, f32[16,128,256]{2,1,0:T(8,128)S(1)}, s32[3,32,2]{1,2,0:T(2,128)S(1)}, bf16[3,32,128,128]{3,2,1,0:T(8,128)(2,1)}, ...), condition=%wide.region_2.3_spmd, body=%wide.region_0.2_spmd.sunk | while | flops 270534016 | bytes 24123028 | solution.py:32
  94.4 3.6 gather_fusion
  98.1 4.6 fusion.38
  102.7 6.5 scatter_fusion
  109.3 3.6 gather_fusion
  112.9 4.6 fusion.38
  117.5 6.5 scatter_fusion
  124.1 3.6 gather_fusion
  127.7 4.6 fusion.38
  132.4 6.5 scatter_fusion
  138.9 0.0 copy-start.3
  138.9 1.1 convert_element_type.26
  140.0 0.0 reduce-scatter.3.cloned.1.call-update
  140.0 0.0 all-gather.5.cloned.1.call-start
  140.1 79.5 %reduce-scatter.3.cloned.1.call-done = bf16[128,256]{1,0:T(8,128)(2,1)} async-done(((bf16[2048,256]{1,0:T(8,128)(2,1)}), bf16[128,256]{1,0:T(8,128)(2,1)}) %reduce-scatter.3.cloned.1.call-update) | async-done | bytes 65552 | tf_op jit(solution)/shard_map/reduce_scatter | solution.py:49
  219.5 0.0 copy-done
  219.5 0.0 copy-done.3
  219.5 1.0 multiply_convert_fusion
  220.6 0.8 convolution_convert_fusion
  221.4 0.0 all-gather.5.cloned.1.call-update
  221.4 0.0 copy-start.2
  221.4 0.0 all-reduce.2.cloned.1.call-start
  221.5 4.7 copy.9
  226.2 0.0 copy-done.2
  226.2 0.9 fusion.20
  227.1 0.0 all-reduce.2.cloned.1.call-update
  227.1 0.0 reduce-scatter.5.cloned.1.call-start
  227.2 79.4 %all-gather.5.cloned.1.call-done = bf16[2048,256]{1,0:T(8,128)(2,1)} async-done(((bf16[128,256]{1,0:T(8,128)(2,1)}), bf16[2048,256]{1,0:T(8,128)(2,1)}) %all-gather.5.cloned.1.call-update) | async-done | bytes 1048592 | tf_op jit(solution)/shard_map/all_gather | solution.py:61
  306.6 0.0 copy-start.1
  306.6 2.4 broadcast_in_dim.28
  309.0 0.0 copy-done.1
  309.0 43.9 %while.21 = (s32[]{:T(128)}, f32[32,128,256]{2,1,0:T(8,128)}, s32[3,32,2]{1,2,0:T(2,128)S(1)}, bf16[3,32,128,128]{2,3,1,0:T(8,128)(2,1)}, bf16[16,128,256]{2,1,0:T(8,128)(2,1)S(1)}, /*index=5*/s32[]{:T(128)}) while((s32[]{:T(128)}, f32[32,128,256]{2,1,0:T(8,128)}, s32[3,32,2]{1,2,0:T(2,128)S(1)}, bf16[3,32,128,128]{2,3,1,0:T(8,128)(2,1)}, ...), condition=%wide.region_6.7_spmd, body=%wide.region_4.6_spmd.sunk | while | flops 270534016 | bytes 24123028 | solution.py:32
  309.0 0.7 gather_fusion.1
  309.7 4.0 fusion.42
  313.7 10.0 %scatter_fusion.1 = f32[32,128,256]{2,1,0:T(8,128)} fusion(f32[32,128,256]{2,1,0:T(8,128)} %get-tuple-element.192, s32[32]{0:T(128)S(1)} %get-tuple-element.165, f32[32,128,256]{2,1,0:T(8,128)} %fusion.42), kind=kCustom, calls=%fused_computation.3.clone.1 | custom fusion | flops 1048576 | bytes 12583040 | tf_op jit(solution)/shard_map/while/body/eval_jaxpr/scatter-add | solution.py:30
  323.8 0.7 gather_fusion.1
  324.5 4.0 fusion.42
  328.4 9.7 %scatter_fusion.1 = f32[32,128,256]{2,1,0:T(8,128)} fusion(f32[32,128,256]{2,1,0:T(8,128)} %get-tuple-element.192, s32[32]{0:T(128)S(1)} %get-tuple-element.165, f32[32,128,256]{2,1,0:T(8,128)} %fusion.42), kind=kCustom, calls=%fused_computation.3.clone.1 | custom fusion | flops 1048576 | bytes 12583040 | tf_op jit(solution)/shard_map/while/body/eval_jaxpr/scatter-add | solution.py:30
  338.2 0.7 gather_fusion.1
  338.9 4.0 fusion.42
  342.9 10.0 %scatter_fusion.1 = f32[32,128,256]{2,1,0:T(8,128)} fusion(f32[32,128,256]{2,1,0:T(8,128)} %get-tuple-element.192, s32[32]{0:T(128)S(1)} %get-tuple-element.165, f32[32,128,256]{2,1,0:T(8,128)} %fusion.42), kind=kCustom, calls=%fused_computation.3.clone.1 | custom fusion | flops 1048576 | bytes 12583040 | tf_op jit(solution)/shard_map/while/body/eval_jaxpr/scatter-add | solution.py:30
  352.9 3.8 convert_element_type.30
  356.7 0.0 reduce-scatter.5.cloned.1.call-update
  356.7 418.6 %all-reduce.2.cloned.1.call-done = f32[256,256]{1,0:T(8,128)} async-done(((f32[256,256]{1,0:T(8,128)}), f32[256,256]{1,0:T(8,128)}) %all-reduce.2.cloned.1.call-update) | async-done | bytes 262160 | tf_op jit(solution)/shard_map/psum | solution.py:68
  775.4 1.7 broadcast_multiply_fusion
  777.0 121.2 %reduce-scatter.5.cloned.1.call-done = bf16[128,256]{1,0:T(8,128)(2,1)} async-done(((bf16[4096,256]{1,0:T(8,128)(2,1)}), bf16[128,256]{1,0:T(8,128)(2,1)}) %reduce-scatter.5.cloned.1.call-update) | async-done | bytes 65552 | tf_op jit(solution)/shard_map/reduce_scatter | solution.py:64
  (25 shorter events, 0.2 us)
Async XLA Ops:
  7.2 212.3 %copy-start = (bf16[256,256]{1,0:T(8,128)(2,1)S(1)}, bf16[256,256]{1,0:T(8,128)(2,1)}, u32[]{:S(2)}) copy-start(bf16[256,256]{1,0:T(8,128)(2,1)} %param.11) | copy-start | bytes 393220
  7.2 87.0 %all-gather.3.cloned.1.call-start = ((), (), s32[]{:S(2)}) async-start(), calls=%async_computation.2 | async-start | bytes 2162688 | tf_op jit(solution)/shard_map/all_gather | solution.py:46
  7.9 211.6 %reduce-scatter.3.cloned.1.call-start = ((), (), s32[]{:S(2)}) async-start(), calls=%async_computation.3 | async-start | bytes 1114112 | tf_op jit(solution)/shard_map/reduce_scatter | solution.py:49
  138.9 80.6 %copy-start.3 = (bf16[128,256]{1,0:T(8,128)(2,1)S(1)}, bf16[128,256]{1,0:T(8,128)(2,1)}, u32[]{:S(2)}) copy-start(bf16[128,256]{1,0:T(8,128)(2,1)} %param.10) | copy-start | bytes 196612
  140.0 166.6 %all-gather.5.cloned.1.call-start = ((), (), s32[]{:S(2)}) async-start(), calls=%async_computation.4 | async-start | bytes 1114112 | tf_op jit(solution)/shard_map/all_gather | solution.py:61
  221.4 4.8 copy-start.2
  221.4 553.9 %all-reduce.2.cloned.1.call-start = ((), (), s32[]{:S(2)}) async-start(), calls=%async_computation.6 | async-start | bytes 524288 | tf_op jit(solution)/shard_map/psum | solution.py:68
  227.1 671.0 %reduce-scatter.5.cloned.1.call-start = ((), (), s32[]{:S(2)}) async-start(), calls=%async_computation.5 | async-start | bytes 2162688 | tf_op jit(solution)/shard_map/reduce_scatter | solution.py:64
  306.6 2.4 copy-start.1
Sparse Core Ops, SparseCore 0:
  11.1 82.9 all-gather.2
  140.1 79.3 reduce-scatter.2
  222.4 84.1 all-gather.4
  313.3 461.9 all-reduce.1
  780.2 117.9 reduce-scatter.4
where the time goes:
time: 906 us; the launch traced here: 905 us
  waiting for transfers between devices  785 us (87%)
  other arithmetic  55.9 us (6%)
  matrix products  28.7 us (3%)
  local copies, waits for them, and re-layouts  21.1 us (2%)
  between operations  13.8 us (2%)
    psum x1, waiting for transfers between devices, on_device(): lax.psum(weight_term, ('row', 'col')) * (1.0 / math.sqrt(nodes))  419 us
    reduce_scatter x1, waiting for transfers between devices, on_device(): lax.psum_scatter(back, 'row', scatter_dimension=0, tiled=True)  121 us
    all_gather x1, waiting for transfers between devices, on_device(): sources = lax.all_gather(features, 'row', axis=0, tiled=True)  85.4 us
    reduce_scatter x1, waiting for transfers between devices, on_device(): lax.psum_scatter(partial_value, 'col', scatter_dimension=0, tiled=True)  79.5 us
    all_gather x1, waiting for transfers between devices, on_device(): node_grad = lax.all_gather(own_grad, 'col', axis=0, tiled=True)  79.4 us
    scatter-add x6, other arithmetic, step(): return (total.at[dst_index].add(product), None)  49.2 us
    dot_general x6, matrix products, step(): jnp.einsum(form, tile_part, picked, preferred_element_type=jnp.float32)  25.9 us
  transfers between devices with their start and end apart: 5, of which 5 were waited for; matrix products, arithmetic and copies ran while one was open for 6% of the time, Pallas kernels for 0%

commit v1 on v0

v1 whole, which is shorter than its diff:
```python
import functools
import math

import jax
import jax.numpy as jnp
from jax import lax
from jax.experimental import pallas as pl
from jax.experimental.pallas import tpu as pltpu
from jax.sharding import Mesh
from jax.sharding import PartitionSpec as P

F32 = jnp.float32
BF16 = jnp.bfloat16
SIZES = {"y": 4, "zh": 4, "co": 2, "x": 4, "zl": 4}
NY, NZH, NCO, NX, NZL = (SIZES[a] for a in ("y", "zh", "co", "x", "zl"))
ROW = ("y", "zh", "co")
COL = ("x", "zl")
T = 128
H = 256
GROUP = 8
VMEM_LIMIT = 40 * 1024 * 1024


def exchange(value, axis):
    return lax.all_to_all(value, axis, 0, 0, tiled=True)


def spread(value, axis):
    return exchange(jnp.broadcast_to(value[None], (SIZES[axis],) + value.shape), axis)


def swap_cores(value):
    return lax.ppermute(value, "co", [(0, 1), (1, 0)])


def split_pair(value):
    high = value.astype(BF16)
    low = (value - high.astype(F32)).astype(BF16)
    return jnp.concatenate([high[:, :T], high[:, T:], low[:, :T], low[:, T:]], axis=0)


def join_pair(rows):
    n = rows.shape[0] // 4
    rows = rows.astype(F32)
    high = jnp.concatenate([rows[:n], rows[n : 2 * n]], axis=1)
    low = jnp.concatenate([rows[2 * n : 3 * n], rows[3 * n :]], axis=1)
    return high + low


def forward_kernel(coords, core, tiles_hbm, own_hbm, other_hbm, out, tiles, source, total, sem, sem_x):
    slots = tiles.shape[0]
    half = own_hbm.shape[0]
    groups = slots // GROUP

    def tile_copy(g):
        at = pl.ds(g * GROUP, GROUP)
        return pltpu.make_async_copy(tiles_hbm.at[at], tiles.at[at], sem.at[g])

    copies = [
        pltpu.make_async_copy(own_hbm, source.at[pl.ds(0, half)], sem_x.at[0]),
        pltpu.make_async_copy(other_hbm, source.at[pl.ds(half, half)], sem_x.at[1]),
    ]
    for c in copies:
        c.start()
    for g in range(groups):
        tile_copy(g).start()
    total[...] = jnp.zeros_like(total)
    me = core[0]
    for c in copies:
        c.wait()

    def step(g, carry):
        tile_copy(g).wait()
        products = []
        for u in range(GROUP):
            k = g * GROUP + u
            j = coords[2 * k + 1]
            at = ((j & 1) ^ me) * half + (j >> 1)
            products.append(jnp.dot(tiles[k], source[at], preferred_element_type=F32))
        for u in range(GROUP):
            i = coords[2 * (g * GROUP + u)]
            total[i] += products[u]
        return carry

    lax.fori_loop(0, groups, step, 0)
    out[...] = total[...].astype(out.dtype)


def dense_kernel(parts, weight, grad_out, out):
    total = parts[0].astype(F32)
    for s in range(1, parts.shape[0]):
        total = total + parts[s].astype(F32)
    aggregated = total.astype(BF16)
    pre = jnp.dot(aggregated, weight[...], preferred_element_type=F32)
    sig = jax.nn.sigmoid(pre)
    slope = grad_out[...].astype(F32) * (sig * (1.0 + pre * (1.0 - sig)))
    slope_t = slope.T.astype(BF16)
    agg_t = aggregated.astype(F32).T.astype(BF16)
    share = H // (NX * NZL)
    for l in range(NZL):
        out[l, :H] = slope_t
        for x in range(NX):
            at = (x * NZL + l) * share
            out[l, H + x * share : H + (x + 1) * share] = agg_t[at : at + share]


def backward_kernel(coords, core, tiles_hbm, grads, weight, mine, other, tiles, source, total, sem):
    slots = tiles.shape[0]
    blocks = grads.shape[0]
    half = total.shape[0] // 2
    groups = slots // GROUP

    def tile_copy(g):
        at = pl.ds(g * GROUP, GROUP)
        return pltpu.make_async_copy(tiles_hbm.at[at], tiles.at[at], sem.at[g])

    for g in range(groups):
        tile_copy(g).start()
    total[...] = jnp.zeros_like(total)
    me = core[0]
    share = grads.shape[1] - H
    weight_grad = jnp.zeros((share, H), F32)
    for c in range(blocks):
        slope_t = grads[c, :H]
        source[c] = jnp.dot(weight[...], slope_t, preferred_element_type=F32).astype(BF16)
        weight_grad = weight_grad + lax.dot_general(
            grads[c, H:], slope_t, (((1,), (1,)), ((), ())), preferred_element_type=F32
        )

    def step(g, carry):
        tile_copy(g).wait()
        products = []
        for u in range(GROUP):
            k = g * GROUP + u
            products.append(jnp.dot(source[coords[2 * k]], tiles[k], preferred_element_type=F32))
        for u in range(GROUP):
            j = coords[2 * (g * GROUP + u) + 1]
            at = ((j & 1) ^ me) * half + (j >> 1)
            total[at] += products[u]
        return carry

    lax.fori_loop(0, groups, step, 0)
    pair = split_pair(weight_grad)
    for value, first in ((mine, 0), (other, half)):
        for p in range(half):
            value[p * H : (p + 1) * H] = total[first + p].astype(BF16)
        value[half * H :] = pair


def core_sum_kernel(mine, other, out):
    rows = (mine.shape[0] - out.shape[1]) // (NY - 1)
    pair = split_pair(join_pair(mine[NY * rows :]) + join_pair(other[NY * rows :]))
    for y in range(NY):
        at = pl.ds(y * rows, rows)
        out[y, :rows] = (mine[at].astype(F32) + other[at].astype(F32)).astype(BF16)
        out[y, rows:] = pair


def y_sum_kernel(parts, out):
    rows = NZH * H
    pair = join_pair(parts[0, rows:])
    for s in range(1, NY):
        pair = pair + join_pair(parts[s, rows:])
    pair = split_pair(pair)
    for z in range(NZH):
        at = pl.ds(z * H, H)
        total = parts[0, at].astype(F32)
        for s in range(1, NY):
            total = total + parts[s, at].astype(F32)
        out[z, :H] = total.astype(BF16)
        out[z, H:] = pair


def last_sum_kernel(parts, out, weight_grad):
    total = parts[0, :H].astype(F32)
    pair = join_pair(parts[0, H:])
    for s in range(1, NZH):
        total = total + parts[s, :H].astype(F32)
        pair = pair + join_pair(parts[s, H:])
    out[...] = total.T.astype(BF16)
    weight_grad[...] = pair


def shape(*dims, dtype=BF16):
    return jax.ShapeDtypeStruct(dims, dtype)


def call(body, outs, ins, flops=0, scratch=(), name=None):
    moved = sum(math.prod(o.shape) * o.dtype.itemsize for o in outs)
    single = len(outs) == 1
    vmem = pl.BlockSpec(memory_space=pltpu.VMEM)
    return pl.pallas_call(
        body,
        out_shape=outs[0] if single else tuple(outs),
        in_specs=[pl.BlockSpec(memory_space=s) for s in ins],
        out_specs=vmem if single else tuple(vmem for _ in outs),
        scratch_shapes=list(scratch),
        compiler_params=pltpu.CompilerParams(vmem_limit_bytes=VMEM_LIMIT),
        cost_estimate=pl.CostEstimate(flops=flops, bytes_accessed=4 * moved, transcendentals=0),
        name=name,
    )


def on_device(features, grad_out, weight, tiles, coords):
    tile_set = tiles[0, 0]
    coord_set = coords[0, 0].reshape(-1)
    slots = tile_set.shape[0]
    groups = slots // GROUP
    core = lax.axis_index("co").astype(jnp.int32).reshape(1)
    nodes = T * math.prod(SIZES.values())
    row_tiles, col_tiles = NX * NZL, NY * NZH * NCO
    half = col_tiles // 2
    share = H // row_tiles
    pair_rows = 4 * share
    SMEM, VMEM, ANY = pltpu.SMEM, pltpu.VMEM, pl.ANY
    product_flops = 2 * slots * T * T * H

    with jax.named_scope("gather_features"):
        own = spread(spread(features, "zh").reshape(NZH, T, H), "y").reshape(half, T, H)
        other = swap_cores(own)
    part = call(
        forward_kernel,
        [shape(row_tiles, T, H)],
        [SMEM, SMEM, ANY, ANY, ANY],
        flops=product_flops,
        scratch=[
            VMEM((slots, T, T), BF16),
            VMEM((col_tiles, T, H), BF16),
            VMEM((row_tiles, T, H), F32),
            pltpu.SemaphoreType.DMA((groups,)),
            pltpu.SemaphoreType.DMA((2,)),
        ],
        name="forward_products",
    )(coord_set, core, tile_set, own, other)
    with jax.named_scope("sum_over_col"):
        part = exchange(part.reshape(NX, NZL, T, H), "x")
        part = jnp.sum(part.astype(F32), axis=0).astype(BF16)
        part = exchange(part, "zl")
    grads = call(
        dense_kernel,
        [shape(NZL, H + NX * share, T)],
        [VMEM] * 3,
        flops=2 * T * H * H,
        name="dense",
    )(part, weight, grad_out)
    with jax.named_scope("gather_gradients"):
        grads = exchange(grads, "zl")
        common = jnp.broadcast_to(grads[None, :, :H], (NX, NZL, H, T))
        slices = grads[:, H:].reshape(NZL, NX, share, T).transpose(1, 0, 2, 3)
        grads = exchange(jnp.concatenate([common, slices], axis=2), "x")
        grads = grads.reshape(row_tiles, H + share, T)
    mine, theirs = call(
        backward_kernel,
        [shape(half * H + pair_rows, T), shape(half * H + pair_rows, T)],
        [SMEM, SMEM, ANY, VMEM, VMEM],
        flops=product_flops,
        scratch=[
            VMEM((slots, T, T), BF16),
            VMEM((row_tiles, H, T), BF16),
            VMEM((col_tiles, H, T), F32),
            pltpu.SemaphoreType.DMA((groups,)),
        ],
        name="backward_products",
    )(coord_set, core, tile_set, grads, weight)
    with jax.named_scope("sum_over_row"):
        theirs = swap_cores(theirs)
        back = call(core_sum_kernel, [shape(NY, NZH * H + pair_rows, T)], [VMEM] * 2, name="core_sum")(
            mine, theirs
        )
        back = exchange(back, "y")
        back = call(y_sum_kernel, [shape(NZH, H + pair_rows, T)], [VMEM], name="y_sum")(back)
        back = exchange(back, "zh")
        grad_features, weight_grad = call(
            last_sum_kernel, [shape(T, H), shape(share, H, dtype=F32)], [VMEM], name="last_sum"
        )(back)
    with jax.named_scope("gather_weight_grad"):
        weight_grad = spread(weight_grad, "zl").reshape(NZL * share, H)
        weight_grad = spread(weight_grad, "x").reshape(H, H)
    return grad_features, weight_grad * (1.0 / math.sqrt(nodes))


def solution(mesh):
    fine = Mesh(mesh.devices.reshape(tuple(SIZES.values())), tuple(SIZES))
    in_specs = (
        P(COL + ROW, None),
        P(ROW + COL, None),
        P(),
        P(ROW, COL, None, None, None),
        P(ROW, COL, None, None),
    )
    out_specs = (P(COL + ROW, None), P())
    return jax.shard_map(
        on_device, mesh=fine, in_specs=in_specs, out_specs=out_specs, check_vma=False
    )
```

time: 906 us -> 203 us (0.22)
  waiting for transfers between devices: 785 us -> 5.36 us
  blocking collectives: 0 us -> 174 us
  other arithmetic: 55.9 us -> 3.02 us
  matrix products: 28.7 us -> 0 us
  local copies, waits for them, and re-layouts: 21.1 us -> 1.46 us
  Pallas kernels: 0 us -> 13.1 us
  between operations: 13.8 us -> 0.75 us
    psum x1 -> x0, waiting for transfers between devices: 419 us -> none  [on_device(): lax.psum(weight_term, ('row', 'col')) * (1.0 / math.sqrt(nodes))]
    reduce_scatter x2 -> x0, waiting for transfers between devices: 201 us -> none  [the longest x1 121 us: on_device(): lax.psum_scatter(back, 'row', scatter_dimension=0, tiled=True)]
    all_to_all x0 -> x10, blocking collectives: none -> 174 us  [exchange(): return lax.all_to_all(value, axis, 0, 0, tiled=True)]
    all_gather x2 -> x0, waiting for transfers between devices: 165 us -> none  [the longest x1 85.4 us: on_device(): sources = lax.all_gather(features, 'row', axis=0, tiled=True)]
    scatter-add x6 -> x0, other arithmetic: 49.2 us -> none  [step(): return (total.at[dst_index].add(product), None)]
    dot_general x9 -> x0, matrix products: 28.7 us -> none  [the longest x6 25.9 us: step(): jnp.einsum(form, tile_part, picked, preferred_element_type=jnp.float32)]
    pallas_call x0 -> x6, Pallas kernels: none -> 13.1 us  [the longest x1 5.93 us: on_device(): call(forward_kernel, [shape(row_tiles, T, H)], [SMEM, SMEM, ANY, ANY, ANY...]
    gather x6 -> x0, local copies, waits for them, and re-layouts: 12.9 us -> none  [step(): picked = jnp.take(blocks, src_index, axis=0)]
  transfers between devices with their start and end apart: 5 -> 2, of which waited for: 5 -> 2; matrix products, arithmetic and copies ran while one was open for 6% -> 0% of each run, Pallas kernels for 0% -> 0%
where the time goes in v1:
time: 203 us; the launch traced here: 202 us
  blocking collectives  174 us (86%)
  Pallas kernels  13.1 us (6%)
  waiting for transfers between devices  5.36 us (3%)
  starting transfers between devices  3.83 us (2%)
  other arithmetic  3.02 us (1%)
    all_to_all x10, blocking collectives, exchange(): return lax.all_to_all(value, axis, 0, 0, tiled=True)  174 us
    pallas_call x1, Pallas kernels, on_device(): call(forward_kernel, [shape(row_tiles, T, H)], [SMEM, SMEM, ANY, ANY, ANY...  5.93 us
    pallas_call x1, Pallas kernels, on_device(): call(backward_kernel, [shape(half * H + pair_rows, T), shape(half * H + p...  5.8 us
    ppermute x2, waiting for transfers between devices, swap_cores(): return lax.ppermute(value, 'co', [(0, 1), (1, 0)])  5.36 us
  transfers between devices with their start and end apart: 2, of which 2 were waited for; matrix products, arithmetic and copies ran while one was open for 0% of the time, Pallas kernels for 0%

profile of v1, /device:TPU:6, one launch (start us, length us, event | category | flops | bytes accessed | tf_op | source)
XLA Modules:
  0.0 202.0 jit_solution(16252060115338591213)
XLA Ops:
  0.6 0.9 broadcast_in_dim.12
  1.5 33.6 %all_to_all.50 = bf16[4,128,256]{2,1,0:T(8,128)(2,1)S(1)} all-to-all(bf16[4,128,256]{2,1,0:T(8,128)(2,1)S(1)} %broadcast_in_dim.12), channel_id=1, replica_groups=mesh['y'=4,'zh'=4,'co'=2,'x'=4,'zl'=4] {'zh'}, dimensions={0} | all-to-all | bytes 524288 | tf_op jit(solution)/shard_map/gather_features/all_to_all | solution.py:25
  35.1 0.0 copy-start
  35.1 0.1 broadcast_in_dim.13
  35.2 0.0 copy-start.3
  35.2 15.5 %all_to_all.51 = bf16[4,4,128,256]{3,2,1,0:T(8,128)(2,1)} all-to-all(bf16[4,4,128,256]{3,2,1,0:T(8,128)(2,1)S(1)} %broadcast_in_dim.13), channel_id=1, replica_groups=mesh['y'=4,'zh'=4,'co'=2,'x'=4,'zl'=4] {'y'}, dimensions={0} | all-to-all | bytes 2097152 | tf_op jit(solution)/shard_map/gather_features/all_to_all | solution.py:25
  50.7 1.9 collective-permute-start
  52.7 0.0 copy-done.3
  52.7 0.1 copy.8
  52.8 0.1 reshape_squeeze.3.coords
  52.9 2.7 %collective-permute-done.other_hbm = bf16[16,128,256]{2,1,0:T(8,128)(2,1)} collective-permute-done((bf16[16,128,256]{2,1,0:T(8,128)(2,1)}, bf16[16,128,256]{2,1,0:T(8,128)(2,1)}, u32[]{:S(2)}, u32[]{:S(2)}) %collective-permute-start) | collective-permute-done | bytes 1048608 | tf_op jit(solution)/shard_map/gather_features/ppermute | solution.py:33
  55.6 0.0 copy-done
  55.6 5.9 %forward_products.1 = bf16[16,128,256]{2,1,0:T(8,128)(2,1)S(1)} custom-call(s32[192]{0:T(256)S(1)} %reshape_squeeze.3.coords, s32[1]{0:T(128)} %bitcast.core, bf16[96,128,128]{2,1,0:T(8,128)(2,1)S(1)} %bitcast.13, bf16[16,128,256]{2,1,0:T(8,128)(2,1)} %bitcast.2.own_hbm, bf16[16,128,256]{2,1,0:T(8,128)(2,1)} %collective-permute-done.other_hbm), custom_call_target="tpu_custom_call" | custom-call | flops 805306368 | bytes 4194304 | tf_op jit(solution)/shard_map/forward_products/pallas_call | solution.py:221
  61.6 18.0 %all_to_all.52 = bf16[4,4,128,256]{3,2,1,0:T(8,128)(2,1)} all-to-all(bf16[4,4,128,256]{3,2,1,0:T(8,128)(2,1)S(1)} %bitcast.16), channel_id=1, replica_groups=mesh['y'=4,'zh'=4,'co'=2,'x'=4,'zl'=4] {'x'}, dimensions={0} | all-to-all | bytes 2097152 | tf_op jit(solution)/shard_map/sum_over_col/all_to_all | solution.py:25
  79.6 0.0 copy-start.1
  79.6 0.0 copy-start.2
  79.6 2.2 %reduce_sum.12 = bf16[4,128,256]{2,1,0:T(8,128)(2,1)} reduce(bf16[4,4,128,256]{3,2,1,0:T(8,128)(2,1)} %all_to_all.52, bf16[]{:T(256)} %constant.9.clone.1), dimensions={0}, to_apply=%region_0.0 | reduce | flops 393216 | bytes 1310722 | tf_op jit(solution)/shard_map/sum_over_col/reduce_sum | solution.py:237
  81.8 16.5 %all_to_all.53.parts = bf16[4,128,256]{2,1,0:T(8,128)(2,1)S(1)} all-to-all(bf16[4,128,256]{2,1,0:T(8,128)(2,1)} %reduce_sum.12), channel_id=1, replica_groups=mesh['y'=4,'zh'=4,'co'=2,'x'=4,'zl'=4] {'zl'}, dimensions={0} | all-to-all | bytes 524288 | tf_op jit(solution)/shard_map/sum_over_col/all_to_all | solution.py:25
  98.3 0.0 copy-done.1
  98.3 0.0 copy-done.2
  98.3 0.3 dense.1
  98.6 11.6 %all_to_all.54 = bf16[4,320,128]{2,1,0:T(8,128)(2,1)S(1)} all-to-all(bf16[4,320,128]{2,1,0:T(8,128)(2,1)S(1)} %dense.1), channel_id=1, replica_groups=mesh['y'=4,'zh'=4,'co'=2,'x'=4,'zl'=4] {'zl'}, dimensions={0} | all-to-all | bytes 655360 | tf_op jit(solution)/shard_map/gather_gradients/all_to_all | solution.py:25
  110.3 0.2 broadcast_in_dim.14
  110.5 0.1 pad_maximum_fusion
  110.6 16.5 %all_to_all.55 = bf16[4,4,272,128]{3,2,1,0:T(8,128)(2,1)S(1)} all-to-all(bf16[4,4,272,128]{3,2,1,0:T(8,128)(2,1)S(1)} %pad_maximum_fusion), channel_id=1, replica_groups=mesh['y'=4,'zh'=4,'co'=2,'x'=4,'zl'=4] {'x'}, dimensions={0} | all-to-all | bytes 2228224 | tf_op jit(solution)/shard_map/gather_gradients/all_to_all | solution.py:25
  127.0 5.8 %backward_products.1 = (bf16[4160,128]{1,0:T(8,128)(2,1)S(1)}, bf16[4160,128]{1,0:T(8,128)(2,1)S(1)}) custom-call(s32[192]{0:T(256)S(1)} %reshape_squeeze.3.coords, s32[1]{0:T(128)} %bitcast.core, bf16[96,128,128]{2,1,0:T(8,128)(2,1)S(1)} %bitcast.14, bf16[16,272,128]{2,1,0:T(8,128)(2,1)S(1)} %bitcast.15, bf16[256,256]{1,0:T(8,128)(2,1)S(1)} %copy-done.1), custom_call_target="tpu_custom_call" | custom-call | flops 805306368 | bytes 8519680 | tf_op jit(solution)/shard_map/backward_products/pallas_call | solution.py:252
  132.8 1.9 collective-permute-start.1
  134.8 2.6 %collective-permute-done.1.other = bf16[4160,128]{1,0:T(8,128)(2,1)S(1)} collective-permute-done((bf16[4160,128]{1,0:T(8,128)(2,1)S(1)}, bf16[4160,128]{1,0:T(8,128)(2,1)S(1)}, u32[]{:S(2)}, u32[]{:S(2)}) %collective-permute-start.1) | collective-permute-done | bytes 1064992 | tf_op jit(solution)/shard_map/sum_over_row/ppermute | solution.py:33
  137.4 0.2 core_sum.1
  137.7 18.8 %all_to_all.56.parts = bf16[4,1088,128]{2,1,0:T(8,128)(2,1)S(1)} all-to-all(bf16[4,1088,128]{2,1,0:T(8,128)(2,1)S(1)} %core_sum.1), channel_id=1, replica_groups=mesh['y'=4,'zh'=4,'co'=2,'x'=4,'zl'=4] {'y'}, dimensions={0} | all-to-all | bytes 2228224 | tf_op jit(solution)/shard_map/sum_over_row/all_to_all | solution.py:25
  156.4 0.1 y_sum.1
  156.6 23.9 %all_to_all.57.parts = bf16[4,320,128]{2,1,0:T(8,128)(2,1)S(1)} all-to-all(bf16[4,320,128]{2,1,0:T(8,128)(2,1)S(1)} %y_sum.1), channel_id=1, replica_groups=mesh['y'=4,'zh'=4,'co'=2,'x'=4,'zl'=4] {'zh'}, dimensions={0} | all-to-all | bytes 655360 | tf_op jit(solution)/shard_map/sum_over_row/all_to_all | solution.py:25
  180.5 0.7 last_sum.1
  181.2 10.9 %all_to_all.58 = f32[4,16,256]{2,1,0:T(8,128)S(1)} all-to-all(f32[4,16,256]{2,1,0:T(8,128)S(1)} %broadcast_in_dim.15), channel_id=1, replica_groups=mesh['y'=4,'zh'=4,'co'=2,'x'=4,'zl'=4] {'zl'}, dimensions={0} | all-to-all | bytes 131072 | tf_op jit(solution)/shard_map/gather_weight_grad/all_to_all | solution.py:25
  192.2 9.1 %all_to_all.59 = f32[4,64,256]{2,1,0:T(8,128)S(1)} all-to-all(f32[4,64,256]{2,1,0:T(8,128)S(1)} %broadcast_in_dim.17), channel_id=1, replica_groups=mesh['y'=4,'zh'=4,'co'=2,'x'=4,'zl'=4] {'x'}, dimensions={0} | all-to-all | bytes 524288 | tf_op jit(solution)/shard_map/gather_weight_grad/all_to_all | solution.py:25
  201.2 0.7 broadcast_multiply_fusion
  (5 shorter events, 0.1 us)
Async XLA Ops:
  35.1 20.5 %copy-start = (bf16[1,1,96,128,128]{4,3,2,1,0:T(8,128)(2,1)S(1)}, bf16[1,1,96,128,128]{4,3,2,1,0:T(8,128)(2,1)}, u32[]{:S(2)}) copy-start(bf16[1,1,96,128,128]{4,3,2,1,0:T(8,128)(2,1)} %param.8) | copy-start | bytes 9437188
  35.2 17.5 %copy-start.3 = (s32[1,1,96,2]{2,3,1,0:T(2,128)S(1)}, s32[1,1,96,2]{2,3,1,0:T(2,128)}, u32[]{:S(2)}) copy-start(s32[1,1,96,2]{2,3,1,0:T(2,128)} %param.9) | copy-start | bytes 2308
  50.7 4.9 %collective-permute-start = (bf16[16,128,256]{2,1,0:T(8,128)(2,1)}, bf16[16,128,256]{2,1,0:T(8,128)(2,1)}, u32[]{:S(2)}, u32[]{:S(2)}) collective-permute-start(bf16[16,128,256]{2,1,0:T(8,128)(2,1)} %bitcast.2.own_hbm), channel_id=1, source_target_pairs={{0,16},{16,0},{1,17},{17,1},{2,18},{18,2},{3,19},{19,3},{4,20},{20... | collective-permute-start | bytes 3145736 | tf_op jit(solution)/shard_map/gather_features/ppermute | solution.py:33
  79.6 18.8 %copy-start.1 = (bf16[256,256]{1,0:T(8,128)(2,1)S(1)}, bf16[256,256]{1,0:T(8,128)(2,1)}, u32[]{:S(2)}) copy-start(bf16[256,256]{1,0:T(8,128)(2,1)} %weight.3) | copy-start | bytes 393220
  79.6 18.8 %copy-start.2 = (bf16[128,256]{1,0:T(8,128)(2,1)S(1)}, bf16[128,256]{1,0:T(8,128)(2,1)}, u32[]{:S(2)}) copy-start(bf16[128,256]{1,0:T(8,128)(2,1)} %grad_out.1) | copy-start | bytes 196612
  132.8 4.6 %collective-permute-start.1 = (bf16[4160,128]{1,0:T(8,128)(2,1)S(1)}, bf16[4160,128]{1,0:T(8,128)(2,1)S(1)}, u32[]{:S(2)}, u32[]{:S(2)}) collective-permute-start(bf16[4160,128]{1,0:T(8,128)(2,1)S(1)} %get-tuple-element.7), channel_id=1, source_target_pairs={{0,16},{16,0},{1,17},{17,1},{2,18},{18,2},{3,19},{19,3},{4,20},{20... | collective-permute-start | bytes 3194888 | tf_op jit(solution)/shard_map/sum_over_row/ppermute | solution.py:33

commit v2 on v1

--- a/solution.py
+++ b/solution.py
@@ -1,4 +1,3 @@
-import functools
 import math
 
 import jax
@@ -17,7 +16,7 @@
 COL = ("x", "zl")
 T = 128
 H = 256
-GROUP = 8
+GROUP = 32
 VMEM_LIMIT = 40 * 1024 * 1024
 
 
@@ -47,30 +46,14 @@
     return high + low
 
 
-def forward_kernel(coords, core, tiles_hbm, own_hbm, other_hbm, out, tiles, source, total, sem, sem_x):
-    slots = tiles.shape[0]
-    half = own_hbm.shape[0]
-    groups = slots // GROUP
-
-    def tile_copy(g):
-        at = pl.ds(g * GROUP, GROUP)
-        return pltpu.make_async_copy(tiles_hbm.at[at], tiles.at[at], sem.at[g])
-
-    copies = [
-        pltpu.make_async_copy(own_hbm, source.at[pl.ds(0, half)], sem_x.at[0]),
-        pltpu.make_async_copy(other_hbm, source.at[pl.ds(half, half)], sem_x.at[1]),
-    ]
-    for c in copies:
-        c.start()
-    for g in range(groups):
-        tile_copy(g).start()
+def forward_kernel(coords, core, tiles, own, other, out, source, total):
+    half = own.shape[0]
+    source[:half] = own[...]
+    source[half:] = other[...]
     total[...] = jnp.zeros_like(total)
     me = core[0]
-    for c in copies:
-        c.wait()
 
     def step(g, carry):
-        tile_copy(g).wait()
         products = []
         for u in range(GROUP):
             k = g * GROUP + u
@@ -82,8 +65,15 @@
             total[i] += products[u]
         return carry
 
-    lax.fori_loop(0, groups, step, 0)
+    lax.fori_loop(0, tiles.shape[0] // GROUP, step, 0)
     out[...] = total[...].astype(out.dtype)
+
+
+def x_sum_kernel(parts, out):
+    total = parts[0].astype(F32)
+    for s in range(1, parts.shape[0]):
+        total = total + parts[s].astype(F32)
+    out[...] = total.astype(BF16)
 
 
 def dense_kernel(parts, weight, grad_out, out):
@@ -104,18 +94,9 @@
             out[l, H + x * share : H + (x + 1) * share] = agg_t[at : at + share]
 
 
-def backward_kernel(coords, core, tiles_hbm, grads, weight, mine, other, tiles, source, total, sem):
-    slots = tiles.shape[0]
+def backward_kernel(coords, core, tiles, grads, weight, mine, other, source, total):
     blocks = grads.shape[0]
     half = total.shape[0] // 2
-    groups = slots // GROUP
-
-    def tile_copy(g):
-        at = pl.ds(g * GROUP, GROUP)
-        return pltpu.make_async_copy(tiles_hbm.at[at], tiles.at[at], sem.at[g])
-
-    for g in range(groups):
-        tile_copy(g).start()
     total[...] = jnp.zeros_like(total)
     me = core[0]
     share = grads.shape[1] - H
@@ -128,7 +109,6 @@
         )
 
     def step(g, carry):
-        tile_copy(g).wait()
         products = []
         for u in range(GROUP):
             k = g * GROUP + u
@@ -139,7 +119,7 @@
             total[at] += products[u]
         return carry
 
-    lax.fori_loop(0, groups, step, 0)
+    lax.fori_loop(0, tiles.shape[0] // GROUP, step, 0)
     pair = split_pair(weight_grad)
     for value, first in ((mine, 0), (other, half)):
         for p in range(half):
@@ -178,7 +158,9 @@
         total = total + parts[s, :H].astype(F32)
         pair = pair + join_pair(parts[s, H:])
     out[...] = total.T.astype(BF16)
-    weight_grad[...] = pair
+    scale = 1.0 / math.sqrt(T * math.prod(SIZES.values()))
+    for c in range(NX * NZL):
+        weight_grad[c] = pair * scale
 
 
 def shape(*dims, dtype=BF16):
@@ -205,14 +187,12 @@
     tile_set = tiles[0, 0]
     coord_set = coords[0, 0].reshape(-1)
     slots = tile_set.shape[0]
-    groups = slots // GROUP
     core = lax.axis_index("co").astype(jnp.int32).reshape(1)
-    nodes = T * math.prod(SIZES.values())
     row_tiles, col_tiles = NX * NZL, NY * NZH * NCO
     half = col_tiles // 2
     share = H // row_tiles
     pair_rows = 4 * share
-    SMEM, VMEM, ANY = pltpu.SMEM, pltpu.VMEM, pl.ANY
+    SMEM, VMEM = pltpu.SMEM, pltpu.VMEM
     product_flops = 2 * slots * T * T * H
 
     with jax.named_scope("gather_features"):
@@ -221,20 +201,14 @@
     part = call(
         forward_kernel,
         [shape(row_tiles, T, H)],
-        [SMEM, SMEM, ANY, ANY, ANY],
+        [SMEM, SMEM, VMEM, VMEM, VMEM],
         flops=product_flops,
-        scratch=[
-            VMEM((slots, T, T), BF16),
-            VMEM((col_tiles, T, H), BF16),
-            VMEM((row_tiles, T, H), F32),
-            pltpu.SemaphoreType.DMA((groups,)),
-            pltpu.SemaphoreType.DMA((2,)),
-        ],
+        scratch=[VMEM((col_tiles, T, H), BF16), VMEM((row_tiles, T, H), F32)],
         name="forward_products",
     )(coord_set, core, tile_set, own, other)
     with jax.named_scope("sum_over_col"):
         part = exchange(part.reshape(NX, NZL, T, H), "x")
-        part = jnp.sum(part.astype(F32), axis=0).astype(BF16)
+        part = call(x_sum_kernel, [shape(NZL, T, H)], [VMEM], name="x_sum")(part)
         part = exchange(part, "zl")
     grads = call(
         dense_kernel,
@@ -252,14 +226,9 @@
     mine, theirs = call(
         backward_kernel,
         [shape(half * H + pair_rows, T), shape(half * H + pair_rows, T)],
-        [SMEM, SMEM, ANY, VMEM, VMEM],
+        [SMEM, SMEM, VMEM, VMEM, VMEM],
         flops=product_flops,
-        scratch=[
-            VMEM((slots, T, T), BF16),
-            VMEM((row_tiles, H, T), BF16),
-            VMEM((col_tiles, H, T), F32),
-            pltpu.SemaphoreType.DMA((groups,)),
-        ],
+        scratch=[VMEM((row_tiles, H, T), BF16), VMEM((col_tiles, H, T), F32)],
         name="backward_products",
     )(coord_set, core, tile_set, grads, weight)
     with jax.named_scope("sum_over_row"):
@@ -271,12 +240,11 @@
         back = call(y_sum_kernel, [shape(NZH, H + pair_rows, T)], [VMEM], name="y_sum")(back)
         back = exchange(back, "zh")
         grad_features, weight_grad = call(
-            last_sum_kernel, [shape(T, H), shape(share, H, dtype=F32)], [VMEM], name="last_sum"
+            last_sum_kernel, [shape(T, H), shape(row_tiles, share, H, dtype=F32)], [VMEM], name="last_sum"
         )(back)
     with jax.named_scope("gather_weight_grad"):
-        weight_grad = spread(weight_grad, "zl").reshape(NZL * share, H)
-        weight_grad = spread(weight_grad, "x").reshape(H, H)
-    return grad_features, weight_grad * (1.0 / math.sqrt(nodes))
+        weight_grad = exchange(weight_grad, COL).reshape(H, H)
+    return grad_features, weight_grad
 
 
 def solution(mesh):

time: 203 us -> 192 us (0.946)
  blocking collectives: 174 us -> 169 us
  Pallas kernels: 13.1 us -> 9.62 us
  other arithmetic: 3.02 us -> 0.09 us
    all_to_all x10 -> x9, blocking collectives: 174 us -> 169 us  [exchange(): return lax.all_to_all(value, axis, 0, 0, tiled=True)]
    reduce_sum x1 -> x0, other arithmetic: 2.2 us -> none  [on_device(): part = jnp.sum(part.astype(F32), axis=0).astype(BF16)]
    pallas_call x2 -> x3, Pallas kernels: 6.67 us -> 4.93 us  [the longest x1 4.06 us: on_device(): call(forward_kernel, [shape(row_tiles, T, H)], [SMEM, SMEM, VMEM, VMEM, V...]
where the time goes in v2:
time: 192 us; the launch traced here: 191 us
  blocking collectives  169 us (88%)
  Pallas kernels  9.62 us (5%)
  waiting for transfers between devices  5.36 us (3%)
  starting transfers between devices  3.83 us (2%)
  local copies, waits for them, and re-layouts  2.14 us (1%)
    all_to_all x9, blocking collectives, exchange(): return lax.all_to_all(value, axis, 0, 0, tiled=True)  169 us
    ppermute x2, waiting for transfers between devices, swap_cores(): return lax.ppermute(value, 'co', [(0, 1), (1, 0)])  5.36 us
    pallas_call x1, Pallas kernels, on_device(): call(forward_kernel, [shape(row_tiles, T, H)], [SMEM, SMEM, VMEM, VMEM, V...  4.06 us
    pallas_call x1, Pallas kernels, on_device(): call(backward_kernel, [shape(half * H + pair_rows, T), shape(half * H + p...  4.03 us
  transfers between devices with their start and end apart: 2, of which 2 were waited for; matrix products, arithmetic and copies ran while one was open for 0% of the time, Pallas kernels for 0%

profile of v2, /device:TPU:6, one launch (start us, length us, event | category | flops | bytes accessed | tf_op | source)
XLA Modules:
  0.0 190.7 jit_solution(7249274746038568886)
XLA Ops:
  0.6 0.9 broadcast_in_dim.6
  1.5 33.6 %all_to_all.45 = bf16[4,128,256]{2,1,0:T(8,128)(2,1)S(1)} all-to-all(bf16[4,128,256]{2,1,0:T(8,128)(2,1)S(1)} %broadcast_in_dim.6), channel_id=1, replica_groups=mesh['y'=4,'zh'=4,'co'=2,'x'=4,'zl'=4] {'zh'}, dimensions={0} | all-to-all | bytes 524288 | tf_op jit(solution)/shard_map/gather_features/all_to_all | solution.py:24
  35.1 0.0 copy-start
  35.1 0.1 broadcast_in_dim.7
  35.2 0.0 copy-start.3
  35.2 15.5 %all_to_all.46 = bf16[4,4,128,256]{3,2,1,0:T(8,128)(2,1)} all-to-all(bf16[4,4,128,256]{3,2,1,0:T(8,128)(2,1)S(1)} %broadcast_in_dim.7), channel_id=1, replica_groups=mesh['y'=4,'zh'=4,'co'=2,'x'=4,'zl'=4] {'y'}, dimensions={0} | all-to-all | bytes 2097152 | tf_op jit(solution)/shard_map/gather_features/all_to_all | solution.py:24
  50.7 1.9 %collective-permute-start = (bf16[16,128,256]{2,1,0:T(8,128)(2,1)}, bf16[16,128,256]{2,1,0:T(8,128)(2,1)}, u32[]{:S(2)}, u32[]{:S(2)}) collective-permute-start(bf16[16,128,256]{2,1,0:T(8,128)(2,1)} %bitcast.2.own), channel_id=1, source_target_pairs={{0,16},{16,0},{1,17},{17,1},{2,18},{18,2},{3,19},{19,3},{4,20},{20... | collective-permute-start | bytes 3145736 | tf_op jit(solution)/shard_map/gather_features/ppermute | solution.py:32
  52.7 0.0 copy-done.3
  52.7 0.1 copy.8
  52.8 0.1 reshape_squeeze.3.coords
  52.9 2.7 %collective-permute-done.other = bf16[16,128,256]{2,1,0:T(8,128)(2,1)} collective-permute-done((bf16[16,128,256]{2,1,0:T(8,128)(2,1)}, bf16[16,128,256]{2,1,0:T(8,128)(2,1)}, u32[]{:S(2)}, u32[]{:S(2)}) %collective-permute-start) | collective-permute-done | bytes 1048608 | tf_op jit(solution)/shard_map/gather_features/ppermute | solution.py:32
  55.6 0.0 copy-done
  55.6 4.1 %forward_products.1 = bf16[16,128,256]{2,1,0:T(8,128)(2,1)S(1)} custom-call(s32[192]{0:T(256)S(1)} %reshape_squeeze.3.coords, s32[1]{0:T(128)} %bitcast.core, bf16[96,128,128]{2,1,0:T(8,128)(2,1)S(1)} %bitcast.12, bf16[16,128,256]{2,1,0:T(8,128)(2,1)} %bitcast.2.own, bf16[16,128,256]{2,1,0:T(8,128)(2,1)} %collective-permute-done.other), custom_call_target="tpu_custom_call" | custom-call | flops 805306368 | bytes 4194304 | tf_op jit(solution)/shard_map/forward_products/pallas_call | solution.py:201
  59.7 17.9 %all_to_all.47.parts = bf16[4,4,128,256]{3,2,1,0:T(8,128)(2,1)S(1)} all-to-all(bf16[4,4,128,256]{3,2,1,0:T(8,128)(2,1)S(1)} %bitcast.15), channel_id=1, replica_groups=mesh['y'=4,'zh'=4,'co'=2,'x'=4,'zl'=4] {'x'}, dimensions={0} | all-to-all | bytes 2097152 | tf_op jit(solution)/shard_map/sum_over_col/all_to_all | solution.py:24
  77.6 0.0 copy-start.1
  77.6 0.0 copy-start.2
  77.6 0.1 x_sum.1
  77.7 16.3 %all_to_all.48.parts = bf16[4,128,256]{2,1,0:T(8,128)(2,1)S(1)} all-to-all(bf16[4,128,256]{2,1,0:T(8,128)(2,1)S(1)} %x_sum.1), channel_id=1, replica_groups=mesh['y'=4,'zh'=4,'co'=2,'x'=4,'zl'=4] {'zl'}, dimensions={0} | all-to-all | bytes 524288 | tf_op jit(solution)/shard_map/sum_over_col/all_to_all | solution.py:24
  94.1 0.0 copy-done.1
  94.1 0.0 copy-done.2
  94.1 0.3 dense.1
  94.4 11.6 %all_to_all.49 = bf16[4,320,128]{2,1,0:T(8,128)(2,1)S(1)} all-to-all(bf16[4,320,128]{2,1,0:T(8,128)(2,1)S(1)} %dense.1), channel_id=1, replica_groups=mesh['y'=4,'zh'=4,'co'=2,'x'=4,'zl'=4] {'zl'}, dimensions={0} | all-to-all | bytes 655360 | tf_op jit(solution)/shard_map/gather_gradients/all_to_all | solution.py:24
  106.0 0.2 broadcast_in_dim.8
  106.2 0.1 pad_maximum_fusion
  106.3 16.4 %all_to_all.50 = bf16[4,4,272,128]{3,2,1,0:T(8,128)(2,1)S(1)} all-to-all(bf16[4,4,272,128]{3,2,1,0:T(8,128)(2,1)S(1)} %pad_maximum_fusion), channel_id=1, replica_groups=mesh['y'=4,'zh'=4,'co'=2,'x'=4,'zl'=4] {'x'}, dimensions={0} | all-to-all | bytes 2228224 | tf_op jit(solution)/shard_map/gather_gradients/all_to_all | solution.py:24
  122.7 4.0 %backward_products.1 = (bf16[4160,128]{1,0:T(8,128)(2,1)S(1)}, bf16[4160,128]{1,0:T(8,128)(2,1)S(1)}) custom-call(s32[192]{0:T(256)S(1)} %reshape_squeeze.3.coords, s32[1]{0:T(128)} %bitcast.core, bf16[96,128,128]{2,1,0:T(8,128)(2,1)S(1)} %bitcast.13, bf16[16,272,128]{2,1,0:T(8,128)(2,1)S(1)} %bitcast.14, bf16[256,256]{1,0:T(8,128)(2,1)S(1)} %copy-done.1), custom_call_target="tpu_custom_call" | custom-call | flops 805306368 | bytes 8519680 | tf_op jit(solution)/shard_map/backward_products/pallas_call | solution.py:226
  126.7 1.9 %collective-permute-start.1 = (bf16[4160,128]{1,0:T(8,128)(2,1)S(1)}, bf16[4160,128]{1,0:T(8,128)(2,1)S(1)}, u32[]{:S(2)}, u32[]{:S(2)}) collective-permute-start(bf16[4160,128]{1,0:T(8,128)(2,1)S(1)} %get-tuple-element.7), channel_id=1, source_target_pairs={{0,16},{16,0},{1,17},{17,1},{2,18},{18,2},{3,19},{19,3},{4,20},{20... | collective-permute-start | bytes 3194888 | tf_op jit(solution)/shard_map/sum_over_row/ppermute | solution.py:32
  128.6 2.6 %collective-permute-done.1.other = bf16[4160,128]{1,0:T(8,128)(2,1)S(1)} collective-permute-done((bf16[4160,128]{1,0:T(8,128)(2,1)S(1)}, bf16[4160,128]{1,0:T(8,128)(2,1)S(1)}, u32[]{:S(2)}, u32[]{:S(2)}) %collective-permute-start.1) | collective-permute-done | bytes 1064992 | tf_op jit(solution)/shard_map/sum_over_row/ppermute | solution.py:32
  131.3 0.2 core_sum.1
  131.5 18.8 %all_to_all.51.parts = bf16[4,1088,128]{2,1,0:T(8,128)(2,1)S(1)} all-to-all(bf16[4,1088,128]{2,1,0:T(8,128)(2,1)S(1)} %core_sum.1), channel_id=1, replica_groups=mesh['y'=4,'zh'=4,'co'=2,'x'=4,'zl'=4] {'y'}, dimensions={0} | all-to-all | bytes 2228224 | tf_op jit(solution)/shard_map/sum_over_row/all_to_all | solution.py:24
  150.3 0.1 y_sum.1
  150.5 24.9 %all_to_all.52.parts = bf16[4,320,128]{2,1,0:T(8,128)(2,1)S(1)} all-to-all(bf16[4,320,128]{2,1,0:T(8,128)(2,1)S(1)} %y_sum.1), channel_id=1, replica_groups=mesh['y'=4,'zh'=4,'co'=2,'x'=4,'zl'=4] {'zh'}, dimensions={0} | all-to-all | bytes 655360 | tf_op jit(solution)/shard_map/sum_over_row/all_to_all | solution.py:24
  175.3 0.7 last_sum.1
  176.1 13.9 %all_to_all.53 = f32[16,16,256]{2,1,0:T(8,128)S(1)} all-to-all(f32[16,16,256]{2,1,0:T(8,128)S(1)} %get-tuple-element.9), channel_id=1, replica_groups=mesh['y'=4,'zh'=4,'co'=2,'x'=4,'zl'=4] {'x','zl'}, dimensions={0} | all-to-all | bytes 524288 | tf_op jit(solution)/shard_map/gather_weight_grad/all_to_all | solution.py:24
  190.0 0.7 copy.13
  (3 shorter events, 0.0 us)
Async XLA Ops:
  35.1 20.5 %copy-start = (bf16[1,1,96,128,128]{4,3,2,1,0:T(8,128)(2,1)S(1)}, bf16[1,1,96,128,128]{4,3,2,1,0:T(8,128)(2,1)}, u32[]{:S(2)}) copy-start(bf16[1,1,96,128,128]{4,3,2,1,0:T(8,128)(2,1)} %param.8) | copy-start | bytes 9437188
  35.2 17.5 %copy-start.3 = (s32[1,1,96,2]{2,3,1,0:T(2,128)S(1)}, s32[1,1,96,2]{2,3,1,0:T(2,128)}, u32[]{:S(2)}) copy-start(s32[1,1,96,2]{2,3,1,0:T(2,128)} %param.9) | copy-start | bytes 2308
  50.7 4.9 %collective-permute-start = (bf16[16,128,256]{2,1,0:T(8,128)(2,1)}, bf16[16,128,256]{2,1,0:T(8,128)(2,1)}, u32[]{:S(2)}, u32[]{:S(2)}) collective-permute-start(bf16[16,128,256]{2,1,0:T(8,128)(2,1)} %bitcast.2.own), channel_id=1, source_target_pairs={{0,16},{16,0},{1,17},{17,1},{2,18},{18,2},{3,19},{19,3},{4,20},{20... | collective-permute-start | bytes 3145736 | tf_op jit(solution)/shard_map/gather_features/ppermute | solution.py:32
  77.6 16.5 %copy-start.1 = (bf16[256,256]{1,0:T(8,128)(2,1)S(1)}, bf16[256,256]{1,0:T(8,128)(2,1)}, u32[]{:S(2)}) copy-start(bf16[256,256]{1,0:T(8,128)(2,1)} %weight.3) | copy-start | bytes 393220
  77.6 16.5 %copy-start.2 = (bf16[128,256]{1,0:T(8,128)(2,1)S(1)}, bf16[128,256]{1,0:T(8,128)(2,1)}, u32[]{:S(2)}) copy-start(bf16[128,256]{1,0:T(8,128)(2,1)} %grad_out.1) | copy-start | bytes 196612
  126.7 4.6 %collective-permute-start.1 = (bf16[4160,128]{1,0:T(8,128)(2,1)S(1)}, bf16[4160,128]{1,0:T(8,128)(2,1)S(1)}, u32[]{:S(2)}, u32[]{:S(2)}) collective-permute-start(bf16[4160,128]{1,0:T(8,128)(2,1)S(1)} %get-tuple-element.7), channel_id=1, source_target_pairs={{0,16},{16,0},{1,17},{17,1},{2,18},{18,2},{3,19},{19,3},{4,20},{20... | collective-permute-start | bytes 3194888 | tf_op jit(solution)/shard_map/sum_over_row/ppermute | solution.py:32

commit v3 on v2

v3 whole, which is shorter than its diff:
```python
import math

import jax
import jax.numpy as jnp
from jax import lax
from jax.experimental import pallas as pl
from jax.experimental.pallas import tpu as pltpu
from jax.sharding import Mesh
from jax.sharding import PartitionSpec as P

F32 = jnp.float32
BF16 = jnp.bfloat16
SIZES = {"y": 4, "zh": 4, "co": 2, "x": 4, "zl": 4}
NY, NZH, NCO, NX, NZL = (SIZES[a] for a in ("y", "zh", "co", "x", "zl"))
N = 4
FAR = N - 1
ROW = ("y", "zh", "co")
COL = ("x", "zl")
T = 128
H = 256
GROUP = 32
VMEM_LIMIT = 20 * 1024 * 1024
VMEM_MOST = 48 * 1024 * 1024


def exchange(value, axis):
    return lax.all_to_all(value, axis, 0, 0, tiled=True)


def spread(value, axis):
    return exchange(jnp.broadcast_to(value[None], (SIZES[axis],) + value.shape), axis)


def swap_cores(value):
    return lax.ppermute(value, "co", [(0, 1), (1, 0)])


def shift(value, axis, distance):
    n = SIZES[axis]
    return lax.ppermute(value, axis, [(i, (i + distance) % n) for i in range(n)])


def place(ahead_y, ahead_zh):
    return jnp.where(ahead_zh == 0, ahead_y, FAR + FAR * ahead_y + ahead_zh)


def split_pair(value):
    high = value.astype(BF16)
    low = (value - high.astype(F32)).astype(BF16)
    return jnp.concatenate([high[:, :T], high[:, T:], low[:, :T], low[:, T:]], axis=0)


def join_pair(rows):
    n = rows.shape[0] // 4
    rows = rows.astype(F32)
    high = jnp.concatenate([rows[:n], rows[n : 2 * n]], axis=1)
    low = jnp.concatenate([rows[2 * n : 3 * n], rows[3 * n :]], axis=1)
    return high + low


def far_copies_kernel(zh, gathered, near1, near2, near3, out_near, out_far):
    for d in range(1, N):
        block = gathered[(zh[0] - d) & FAR]
        for y in range(N):
            out_far[y, d - 1] = block
    out_near[0] = gathered[zh[0]]
    for y, near in enumerate((near1, near2, near3), 1):
        out_near[y] = near[...]


def forward_kernel(
    coords, core, y, zh, tiles_hbm, near, far, near_other, far_other, out, tiles, source, total, arrived
):
    groups = tiles.shape[0] // GROUP

    def fetch(g):
        at = pl.ds(g * GROUP, GROUP)
        return pltpu.make_async_copy(tiles_hbm.at[at], tiles.at[at], arrived.at[g])

    for g in range(groups):
        fetch(g).start()
    half = source.shape[0] // 2
    for c, (a, b) in enumerate(((near, far), (near_other, far_other))):
        first = c * half
        source[first : first + N] = a[...]
        for i in range(N):
            at = first + N + i * FAR
            source[at : at + FAR] = b[i]
    total[...] = jnp.zeros_like(total)
    me, my_y, my_zh = core[0], y[0], zh[0]

    def step(g, carry):
        fetch(g).wait()
        products = []
        for u in range(GROUP):
            k = g * GROUP + u
            j = coords[2 * k + 1]
            ahead = (my_zh - (j >> 1)) & FAR
            behind_y = jnp.where(ahead == 0, (my_y - (j >> 3)) & FAR, j >> 3)
            at = ((j & 1) ^ me) * half + place(behind_y, ahead)
            products.append(jnp.dot(tiles[k], source[at], preferred_element_type=F32))
        for u in range(GROUP):
            i = coords[2 * (g * GROUP + u)]
            total[i] += products[u]
        return carry

    lax.fori_loop(0, groups, step, 0)
    out[...] = total[...].astype(out.dtype)


def x_sum_kernel(parts, out):
    total = parts[0].astype(F32)
    for s in range(1, parts.shape[0]):
        total = total + parts[s].astype(F32)
    out[...] = total.astype(BF16)


def dense_kernel(parts, weight, grad_out, out):
    total = parts[0].astype(F32)
    for s in range(1, parts.shape[0]):
        total = total + parts[s].astype(F32)
    aggregated = total.astype(BF16)
    pre = jnp.dot(aggregated, weight[...], preferred_element_type=F32)
    sig = jax.nn.sigmoid(pre)
    slope = grad_out[...].astype(F32) * (sig * (1.0 + pre * (1.0 - sig)))
    slope_t = slope.T.astype(BF16)
    agg_t = aggregated.astype(F32).T.astype(BF16)
    share = H // (NX * NZL)
    for l in range(NZL):
        out[l, :H] = slope_t
        for x in range(NX):
            at = (x * NZL + l) * share
            out[l, H + x * share : H + (x + 1) * share] = agg_t[at : at + share]


def backward_kernel(
    coords, core, y, zh, tiles, grads, weight, mine_near, mine_far, other_near, other_far, source, total
):
    blocks = grads.shape[0]
    half = total.shape[0] // 2
    total[...] = jnp.zeros_like(total)
    me, my_y, my_zh = core[0], y[0], zh[0]
    share = grads.shape[1] - H
    weight_grad = jnp.zeros((share, H), F32)
    for c in range(blocks):
        slope_t = grads[c, :H]
        source[c] = jnp.dot(weight[...], slope_t, preferred_element_type=F32).astype(BF16)
        weight_grad = weight_grad + lax.dot_general(
            grads[c, H:], slope_t, (((1,), (1,)), ((), ())), preferred_element_type=F32
        )

    def step(g, carry):
        products = []
        for u in range(GROUP):
            k = g * GROUP + u
            products.append(jnp.dot(source[coords[2 * k]], tiles[k], preferred_element_type=F32))
        for u in range(GROUP):
            j = coords[2 * (g * GROUP + u) + 1]
            ahead = ((j >> 1) - my_zh) & FAR
            ahead_y = jnp.where(ahead == 0, ((j >> 3) - my_y) & FAR, j >> 3)
            at = ((j & 1) ^ me) * half + place(ahead_y, ahead)
            total[at] += products[u]
        return carry

    lax.fori_loop(0, tiles.shape[0] // GROUP, step, 0)
    pair = split_pair(weight_grad)
    rows = FAR * H
    for first, near, far in ((0, mine_near, mine_far), (half, other_near, other_far)):
        for i in range(N):
            near[i] = total[first + i].astype(BF16)
            for d in range(FAR):
                at = i * rows + d * H
                far[at : at + H] = total[first + N + i * FAR + d].astype(BF16)
        far[N * rows :] = pair


def core_sum_kernel(mine, other, out):
    rows = FAR * H
    pair = split_pair(join_pair(mine[N * rows :]) + join_pair(other[N * rows :]))
    for y in range(N):
        at = pl.ds(y * rows, rows)
        out[y, :rows] = (mine[at].astype(F32) + other[at].astype(F32)).astype(BF16)
        out[y, rows:] = pair


def near_sum_kernel(mine, other, *outs):
    for d, out in enumerate(outs):
        out[...] = (mine[d].astype(F32) + other[d].astype(F32)).astype(BF16)


def y_sum_kernel(zh, parts, out):
    rows = FAR * H
    grad = join_pair(parts[0, rows:])
    for s in range(1, N):
        grad = grad + join_pair(parts[s, rows:])
    grad = jnp.concatenate([grad[:, :T], grad[:, T:]], axis=0).astype(BF16)
    for d in range(N):
        to = (zh[0] + d) & FAR
        if d == 0:
            out[to, :H] = jnp.zeros((H, T), BF16)
        else:
            at = pl.ds((d - 1) * H, H)
            total = parts[0, at].astype(F32)
            for s in range(1, N):
                total = total + parts[s, at].astype(F32)
            out[to, :H] = total.astype(BF16)
        out[to, H:] = grad


def last_sum_kernel(parts, near0, near1, near2, near3, out, weight_grad):
    total = near0[...].astype(F32)
    for near in (near1, near2, near3):
        total = total + near[...].astype(F32)
    grad = jnp.zeros((parts.shape[1] - H, T), F32)
    for s in range(N):
        total = total + parts[s, :H].astype(F32)
        grad = grad + parts[s, H:].astype(F32)
    out[...] = total.T.astype(BF16)
    share = grad.shape[0] // 2
    scale = 1.0 / math.sqrt(T * math.prod(SIZES.values()))
    grad = jnp.concatenate([grad[:share], grad[share:]], axis=1) * scale
    for c in range(NX * NZL):
        weight_grad[c] = grad.astype(BF16)


def shape(*dims, dtype=BF16):
    return jax.ShapeDtypeStruct(dims, dtype)


def call(body, outs, ins, flops=0, scratch=(), name=None, limit=VMEM_LIMIT):
    moved = sum(math.prod(o.shape) * o.dtype.itemsize for o in outs)
    single = len(outs) == 1
    vmem = pl.BlockSpec(memory_space=pltpu.VMEM)
    return pl.pallas_call(
        body,
        out_shape=outs[0] if single else tuple(outs),
        in_specs=[pl.BlockSpec(memory_space=s) for s in ins],
        out_specs=vmem if single else tuple(vmem for _ in outs),
        scratch_shapes=list(scratch),
        compiler_params=pltpu.CompilerParams(vmem_limit_bytes=limit),
        cost_estimate=pl.CostEstimate(flops=flops, bytes_accessed=4 * moved, transcendentals=0),
        name=name,
    )


def on_device(features, grad_out, weight, tiles, coords):
    tile_set = tiles[0, 0]
    coord_set = coords[0, 0].reshape(-1)
    slots = tile_set.shape[0]
    core, y, zh = (lax.axis_index(a).astype(jnp.int32).reshape(1) for a in ("co", "y", "zh"))
    row_tiles, col_tiles = NX * NZL, NY * NZH * NCO
    share = H // row_tiles
    pair_rows = 4 * share
    SMEM, VMEM = pltpu.SMEM, pltpu.VMEM
    product_flops = 2 * slots * T * T * H

    with jax.named_scope("gather_features"):
        gathered = spread(features, "zh").reshape(N, T, H)
        near = [shift(features, "y", d) for d in range(1, N)]
        near, far = call(
            far_copies_kernel,
            [shape(N, T, H), shape(N, FAR, T, H)],
            [SMEM] + [VMEM] * N,
            name="far_copies",
        )(zh, gathered, *near)
        near_other = swap_cores(near)
        far = exchange(far, "y")
        near_other, far = lax.optimization_barrier((near_other, far))
        far_other = swap_cores(far)
    part = call(
        forward_kernel,
        [shape(row_tiles, T, H)],
        [SMEM] * 4 + [pltpu.HBM] + [VMEM] * 4,
        flops=product_flops,
        scratch=[
            VMEM((slots, T, T), BF16),
            VMEM((col_tiles, T, H), BF16),
            VMEM((row_tiles, T, H), F32),
            pltpu.SemaphoreType.DMA((slots // GROUP,)),
        ],
        name="forward_products",
        limit=VMEM_MOST,
    )(coord_set, core, y, zh, tile_set, near, far, near_other, far_other)
    with jax.named_scope("sum_over_col"):
        part = exchange(part.reshape(NX, NZL, T, H), "x")
        part = call(x_sum_kernel, [shape(NZL, T, H)], [VMEM], name="x_sum")(part)
        part = exchange(part, "zl")
    grads = call(
        dense_kernel,
        [shape(NZL, H + NX * share, T)],
        [VMEM] * 3,
        flops=2 * T * H * H,
        name="dense",
    )(part, weight, grad_out)
    with jax.named_scope("gather_gradients"):
        grads = exchange(grads, "zl")
        common = jnp.broadcast_to(grads[None, :, :H], (NX, NZL, H, T))
        slices = grads[:, H:].reshape(NZL, NX, share, T).transpose(1, 0, 2, 3)
        grads = exchange(jnp.concatenate([common, slices], axis=2), "x")
        grads = grads.reshape(row_tiles, H + share, T)
    rows = FAR * H
    outs = [shape(N, H, T), shape(N * rows + pair_rows, T)]
    mine_near, mine_far, other_near, other_far = call(
        backward_kernel,
        outs + outs,
        [SMEM] * 4 + [VMEM] * 3,
        flops=product_flops,
        scratch=[VMEM((row_tiles, H, T), BF16), VMEM((col_tiles, H, T), F32)],
        name="backward_products",
    )(coord_set, core, y, zh, tile_set, grads, weight)
    with jax.named_scope("sum_over_row"):
        other_far = swap_cores(other_far)
        far = call(core_sum_kernel, [shape(N, rows + pair_rows, T)], [VMEM] * 2, name="core_sum")(mine_far, other_far)
        far = exchange(far, "y")
        other_near = swap_cores(other_near)
        near = call(near_sum_kernel, [shape(H, T)] * N, [VMEM] * 2, name="near_sum")(mine_near, other_near)
        far = call(y_sum_kernel, [shape(N, H + 2 * share, T)], [SMEM, VMEM], name="y_sum")(zh, far)
        far = exchange(far, "zh")
        near = [near[0]] + [shift(near[d], "y", d) for d in range(1, N)]
        grad_features, weight_grad = call(
            last_sum_kernel,
            [shape(T, H), shape(row_tiles, share, H)],
            [VMEM] * 5,
            name="last_sum",
        )(far, *near)
    with jax.named_scope("gather_weight_grad"):
        weight_grad = exchange(weight_grad, COL).reshape(H, H).astype(F32)
    return grad_features, weight_grad


def solution(mesh):
    fine = Mesh(mesh.devices.reshape(tuple(SIZES.values())), tuple(SIZES))
    in_specs = (
        P(COL + ROW, None),
        P(ROW + COL, None),
        P(),
        P(ROW, COL, None, None, None),
        P(ROW, COL, None, None),
    )
    out_specs = (P(COL + ROW, None), P())
    return jax.shard_map(
        on_device, mesh=fine, in_specs=in_specs, out_specs=out_specs, check_vma=False
    )
```

time: 192 us -> 187 us (0.974)
  blocking collectives: 169 us -> 91.9 us
  starting transfers between devices: 3.83 us -> 53.1 us
  waiting for transfers between devices: 5.36 us -> 25.1 us
    all_to_all x9 -> x6, blocking collectives: 169 us -> 91.9 us  [exchange(): return lax.all_to_all(value, axis, 0, 0, tiled=True)]
    all_to_all x0 -> x3, starting transfers between devices: none -> 25 us  [exchange(): return lax.all_to_all(value, axis, 0, 0, tiled=True)]
    ppermute x0 -> x6, starting transfers between devices: none -> 20.4 us  [shift(): lax.ppermute(value, axis, [(i, (i + distance) % n) for i in range(n)])]
    all_to_all x0 -> x3, waiting for transfers between devices: none -> 10.6 us  [exchange(): return lax.all_to_all(value, axis, 0, 0, tiled=True)]
    ppermute x0 -> x6, waiting for transfers between devices: none -> 7.19 us  [shift(): lax.ppermute(value, axis, [(i, (i + distance) % n) for i in range(n)])]
    ppermute x2 -> x4, starting transfers between devices: 3.83 us -> 7.65 us  [swap_cores(): return lax.ppermute(value, 'co', [(0, 1), (1, 0)])]
    ppermute x2 -> x4, waiting for transfers between devices: 5.36 us -> 7.27 us  [swap_cores(): return lax.ppermute(value, 'co', [(0, 1), (1, 0)])]
    pallas_call x5 -> x7, Pallas kernels: 9.21 us -> 10.9 us  [the longest x1 4.06 us: on_device(): call(forward_kernel, [shape(row_tiles, T, H)], [SMEM] * 4 + [pltpu.HBM] +...]
  transfers between devices with their start and end apart: 2 -> 13, of which waited for: 2 -> 10; matrix products, arithmetic and copies ran while one was open for 0% -> 0% of each run, Pallas kernels for 0% -> 0%
where the time goes in v3:
time: 187 us; the launch traced here: 185 us
  blocking collectives  91.9 us (49%)
  starting transfers between devices  53.1 us (28%)
  waiting for transfers between devices  25.1 us (13%)
  Pallas kernels  11.3 us (6%)
  local copies, waits for them, and re-layouts  2.05 us (1%)
    all_to_all x6, blocking collectives, exchange(): return lax.all_to_all(value, axis, 0, 0, tiled=True)  91.9 us
    all_to_all x3, starting transfers between devices, exchange(): return lax.all_to_all(value, axis, 0, 0, tiled=True)  25 us
    ppermute x6, starting transfers between devices, shift(): lax.ppermute(value, axis, [(i, (i + distance) % n) for i in range(n)])  20.4 us
    all_to_all x3, waiting for transfers between devices, exchange(): return lax.all_to_all(value, axis, 0, 0, tiled=True)  10.6 us
    ppermute x4, starting transfers between devices, swap_cores(): return lax.ppermute(value, 'co', [(0, 1), (1, 0)])  7.65 us
    ppermute x4, waiting for transfers between devices, swap_cores(): return lax.ppermute(value, 'co', [(0, 1), (1, 0)])  7.27 us
    ppermute x6, waiting for transfers between devices, shift(): lax.ppermute(value, axis, [(i, (i + distance) % n) for i in range(n)])  7.19 us
    pallas_call x1, Pallas kernels, on_device(): call(forward_kernel, [shape(row_tiles, T, H)], [SMEM] * 4 + [pltpu.HBM] +...  4.06 us
  transfers between devices with their start and end apart: 13, of which 10 were waited for; matrix products, arithmetic and copies ran while one was open for 0% of the time, Pallas kernels for 0%

profile of v3, /device:TPU:6, one launch (start us, length us, event | category | flops | bytes accessed | tf_op | source)
XLA Modules:
  0.0 185.1 jit_solution(10166914713105797906)
XLA Ops:
  0.6 1.6 broadcast_in_dim.4
  2.2 15.1 %all-to-all-start = ((bf16[4,128,256]{2,1,0:T(8,128)(2,1)}), bf16[4,128,256]{2,1,0:T(8,128)(2,1)S(1)}, u32[]{:S(2)}, u32[]{:S(2)}) async-start(bf16[4,128,256]{2,1,0:T(8,128)(2,1)} %broadcast_in_dim.4), calls=%async_computation | async-start | bytes 524288 | tf_op jit(solution)/shard_map/gather_features/all_to_all | solution.py:27
  17.3 0.0 copy-start.3
  17.3 3.6 %collective-permute-start = (bf16[128,256]{1,0:T(8,128)(2,1)}, bf16[128,256]{1,0:T(8,128)(2,1)S(1)}, u32[]{:S(2)}, u32[]{:S(2)}) collective-permute-start(bf16[128,256]{1,0:T(8,128)(2,1)} %param.5), channel_id=1, source_target_pairs={{0,128},{128,256},{256,384},{384,0},{1,129},{129,257},{257,385},{3... | collective-permute-start | bytes 196616 | tf_op jit(solution)/shard_map/gather_features/ppermute | solution.py:40
  20.9 3.6 %collective-permute-start.2 = (bf16[128,256]{1,0:T(8,128)(2,1)}, bf16[128,256]{1,0:T(8,128)(2,1)S(1)}, u32[]{:S(2)}, u32[]{:S(2)}) collective-permute-start(bf16[128,256]{1,0:T(8,128)(2,1)} %param.5), channel_id=1, source_target_pairs={{0,384},{128,0},{256,128},{384,256},{1,385},{129,1},{257,129},{385... | collective-permute-start | bytes 196616 | tf_op jit(solution)/shard_map/gather_features/ppermute | solution.py:40
  24.5 3.9 %collective-permute-start.1 = (bf16[128,256]{1,0:T(8,128)(2,1)}, bf16[128,256]{1,0:T(8,128)(2,1)S(1)}, u32[]{:S(2)}, u32[]{:S(2)}) collective-permute-start(bf16[128,256]{1,0:T(8,128)(2,1)} %param.5), channel_id=1, source_target_pairs={{0,256},{128,384},{256,0},{384,128},{1,257},{129,385},{257,1},{385... | collective-permute-start | bytes 196616 | tf_op jit(solution)/shard_map/gather_features/ppermute | solution.py:40
  28.4 0.0 collective-permute-done.near1
  28.4 0.0 collective-permute-done.2.near3
  28.4 3.9 %collective-permute-done.1.near2 = bf16[128,256]{1,0:T(8,128)(2,1)S(1)} collective-permute-done((bf16[128,256]{1,0:T(8,128)(2,1)}, bf16[128,256]{1,0:T(8,128)(2,1)S(1)}, u32[]{:S(2)}, u32[]{:S(2)}) %collective-permute-start.1) | collective-permute-done | bytes 65568 | tf_op jit(solution)/shard_map/gather_features/ppermute | solution.py:40
  32.3 3.5 %all-to-all-done.gathered = bf16[4,128,256]{2,1,0:T(8,128)(2,1)S(1)} async-done(((bf16[4,128,256]{2,1,0:T(8,128)(2,1)}), bf16[4,128,256]{2,1,0:T(8,128)(2,1)S(1)}, u32[]{:S(2)}, u32[]{:S(2)}) %all-to-all-start) | async-done | bytes 262176 | tf_op jit(solution)/shard_map/gather_features/all_to_all | solution.py:27
  35.8 1.0 far_copies.1
  36.8 4.5 %all-to-all-start.1 = ((bf16[4,3,128,256]{3,2,1,0:T(8,128)(2,1)}), bf16[4,3,128,256]{3,2,1,0:T(8,128)(2,1)S(1)}, u32[]{:S(2)}, u32[]{:S(2)}) async-start(bf16[4,3,128,256]{3,2,1,0:T(8,128)(2,1)} %get-tuple-element.17), calls=%async_computation.1 | async-start | bytes 1572864 | tf_op jit(solution)/shard_map/gather_features/all_to_all | solution.py:27
  41.3 1.9 %collective-permute-start.3 = (bf16[4,128,256]{2,1,0:T(8,128)(2,1)S(1)}, bf16[4,128,256]{2,1,0:T(8,128)(2,1)S(1)}, u32[]{:S(2)}, u32[]{:S(2)}) collective-permute-start(bf16[4,128,256]{2,1,0:T(8,128)(2,1)S(1)} %get-tuple-element.16.near), channel_id=1, source_target_pairs={{0,16},{16,0},{1,17},{17,1},{2,18},{18,2},{3,19},{19,3},{4,20},{20... | collective-permute-start | bytes 786440 | tf_op jit(solution)/shard_map/gather_features/ppermute | solution.py:35
  43.2 1.5 collective-permute-done.3.near_other
  44.7 6.1 %all-to-all-done.1.far = bf16[4,3,128,256]{3,2,1,0:T(8,128)(2,1)S(1)} async-done(((bf16[4,3,128,256]{3,2,1,0:T(8,128)(2,1)}), bf16[4,3,128,256]{3,2,1,0:T(8,128)(2,1)S(1)}, u32[]{:S(2)}, u32[]{:S(2)}) %all-to-all-start.1) | async-done | bytes 786464 | tf_op jit(solution)/shard_map/gather_features/all_to_all | solution.py:27
  50.7 1.9 %collective-permute-start.4 = (bf16[4,3,128,256]{3,2,1,0:T(8,128)(2,1)S(1)}, bf16[4,3,128,256]{3,2,1,0:T(8,128)(2,1)S(1)}, u32[]{:S(2)}, u32[]{:S(2)}) collective-permute-start(bf16[4,3,128,256]{3,2,1,0:T(8,128)(2,1)S(1)} %all-to-all-done.1.far), channel_id=1, source_target_pairs={{0,16},{16,0},{1,17},{17,1},{2,18},{18,2},{3,19},{19,3},{4,20},{20... | collective-permute-start | bytes 2359304 | tf_op jit(solution)/shard_map/gather_features/ppermute | solution.py:35
  52.7 0.0 copy-done.3
  52.7 0.1 copy.8
  52.8 0.1 reshape_squeeze.3.coords
  52.9 2.0 %collective-permute-done.4.far_other = bf16[4,3,128,256]{3,2,1,0:T(8,128)(2,1)S(1)} collective-permute-done((bf16[4,3,128,256]{3,2,1,0:T(8,128)(2,1)S(1)}, bf16[4,3,128,256]{3,2,1,0:T(8,128)(2,1)S(1)}, u32[]{:S(2)}, u32[]{:S(2)}) %collective-permute-start.4) | collective-permute-done | bytes 786464 | tf_op jit(solution)/shard_map/gather_features/ppermute | solution.py:35
  54.9 4.1 %forward_products.1 = bf16[16,128,256]{2,1,0:T(8,128)(2,1)S(1)} custom-call(s32[192]{0:T(256)S(1)} %reshape_squeeze.3.coords, s32[1]{0:T(128)} %bitcast.1.core, s32[1]{0:T(128)} %bitcast.2.y, s32[1]{0:T(128)} %bitcast.zh, bf16[96,128,128]{2,1,0:T(8,128)(2,1)} %bitcast.15, bf16[4,128,256]{2,1,0:T(8,128)(2,1)S(1)} %get-tuple-element.16.near, ...), custom_call_target="tpu_custom_call" | custom-call | flops 805306368 | bytes 4194304 | tf_op jit(solution)/shard_map/forward_products/pallas_call | solution.py:270
  59.0 17.9 %all_to_all.45.parts = bf16[4,4,128,256]{3,2,1,0:T(8,128)(2,1)S(1)} all-to-all(bf16[4,4,128,256]{3,2,1,0:T(8,128)(2,1)S(1)} %bitcast.18), channel_id=1, replica_groups=mesh['y'=4,'zh'=4,'co'=2,'x'=4,'zl'=4] {'x'}, dimensions={0} | all-to-all | bytes 2097152 | tf_op jit(solution)/shard_map/sum_over_col/all_to_all | solution.py:27
  76.9 0.0 copy-start.1
  76.9 0.0 copy-start.2
  76.9 0.1 x_sum.1
  77.0 13.8 %all_to_all.46.parts = bf16[4,128,256]{2,1,0:T(8,128)(2,1)S(1)} all-to-all(bf16[4,128,256]{2,1,0:T(8,128)(2,1)S(1)} %x_sum.1), channel_id=1, replica_groups=mesh['y'=4,'zh'=4,'co'=2,'x'=4,'zl'=4] {'zl'}, dimensions={0} | all-to-all | bytes 524288 | tf_op jit(solution)/shard_map/sum_over_col/all_to_all | solution.py:27
  90.9 0.0 copy-done.1
  90.9 0.0 copy-done.2
  90.9 0.3 dense.1
  91.2 11.6 %all_to_all.47 = bf16[4,320,128]{2,1,0:T(8,128)(2,1)S(1)} all-to-all(bf16[4,320,128]{2,1,0:T(8,128)(2,1)S(1)} %dense.1), channel_id=1, replica_groups=mesh['y'=4,'zh'=4,'co'=2,'x'=4,'zl'=4] {'zl'}, dimensions={0} | all-to-all | bytes 655360 | tf_op jit(solution)/shard_map/gather_gradients/all_to_all | solution.py:27
  102.8 0.2 broadcast_in_dim.5
  103.0 0.0 copy-start
  103.0 0.1 pad_maximum_fusion
  103.1 16.7 %all_to_all.48 = bf16[4,4,272,128]{3,2,1,0:T(8,128)(2,1)S(1)} all-to-all(bf16[4,4,272,128]{3,2,1,0:T(8,128)(2,1)S(1)} %pad_maximum_fusion), channel_id=1, replica_groups=mesh['y'=4,'zh'=4,'co'=2,'x'=4,'zl'=4] {'x'}, dimensions={0} | all-to-all | bytes 2228224 | tf_op jit(solution)/shard_map/gather_gradients/all_to_all | solution.py:27
  119.7 0.0 copy-done
  119.7 4.0 %backward_products.1 = (bf16[4,256,128]{2,1,0:T(8,128)(2,1)S(1)}, bf16[3136,128]{1,0:T(8,128)(2,1)S(1)}, bf16[4,256,128]{2,1,0:T(8,128)(2,1)S(1)}, bf16[3136,128]{1,0:T(8,128)(2,1)S(1)}) custom-call(s32[192]{0:T(256)S(1)} %reshape_squeeze.3.coords, s32[1]{0:T(128)} %bitcast.1.core, s32[1]{0:T(128)} %bitcast.2.y, s32[1]{0:T(128)} %bitcast.zh, ...), custom_call_target="tpu_custom_call" | custom-call | flops 805306368 | bytes 8519680 | tf_op jit(solution)/shard_map/backward_products/pallas_call | solution.py:303
  123.8 1.9 %collective-permute-start.5 = (bf16[3136,128]{1,0:T(8,128)(2,1)S(1)}, bf16[3136,128]{1,0:T(8,128)(2,1)S(1)}, u32[]{:S(2)}, u32[]{:S(2)}) collective-permute-start(bf16[3136,128]{1,0:T(8,128)(2,1)S(1)} %get-tuple-element.21), channel_id=1, source_target_pairs={{0,16},{16,0},{1,17},{17,1},{2,18},{18,2},{3,19},{19,3},{4,20},{20... | collective-permute-start | bytes 2408456 | tf_op jit(solution)/shard_map/sum_over_row/ppermute | solution.py:35
  125.7 2.3 %collective-permute-done.5.other = bf16[3136,128]{1,0:T(8,128)(2,1)S(1)} collective-permute-done((bf16[3136,128]{1,0:T(8,128)(2,1)S(1)}, bf16[3136,128]{1,0:T(8,128)(2,1)S(1)}, u32[]{:S(2)}, u32[]{:S(2)}) %collective-permute-start.5) | collective-permute-done | bytes 802848 | tf_op jit(solution)/shard_map/sum_over_row/ppermute | solution.py:35
  128.0 0.2 core_sum.1
  128.2 16.0 %all_to_all.49.parts = bf16[4,832,128]{2,1,0:T(8,128)(2,1)S(1)} all-to-all(bf16[4,832,128]{2,1,0:T(8,128)(2,1)S(1)} %core_sum.1), channel_id=1, replica_groups=mesh['y'=4,'zh'=4,'co'=2,'x'=4,'zl'=4] {'y'}, dimensions={0} | all-to-all | bytes 1703936 | tf_op jit(solution)/shard_map/sum_over_row/all_to_all | solution.py:27
  144.1 0.8 y_sum.1
  145.0 5.5 %all-to-all-start.7 = ((bf16[4,288,128]{2,1,0:T(8,128)(2,1)}), bf16[4,288,128]{2,1,0:T(8,128)(2,1)S(1)}, u32[]{:S(2)}, u32[]{:S(2)}) async-start(bf16[4,288,128]{2,1,0:T(8,128)(2,1)} %y_sum.1), calls=%async_computation.7 | async-start | bytes 589824 | tf_op jit(solution)/shard_map/sum_over_row/all_to_all | solution.py:27
  150.4 1.9 %collective-permute-start.6 = (bf16[4,256,128]{2,1,0:T(8,128)(2,1)S(1)}, bf16[4,256,128]{2,1,0:T(8,128)(2,1)S(1)}, u32[]{:S(2)}, u32[]{:S(2)}) collective-permute-start(bf16[4,256,128]{2,1,0:T(8,128)(2,1)S(1)} %get-tuple-element.23), channel_id=1, source_target_pairs={{0,16},{16,0},{1,17},{17,1},{2,18},{18,2},{3,19},{19,3},{4,20},{20... | collective-permute-start | bytes 786440 | tf_op jit(solution)/shard_map/sum_over_row/ppermute | solution.py:35
  152.3 1.5 collective-permute-done.6.other
  153.9 0.1 near_sum.1
  153.9 2.5 %collective-permute-start.7 = (bf16[256,128]{1,0:T(8,128)(2,1)S(1)}, bf16[256,128]{1,0:T(8,128)(2,1)S(1)}, u32[]{:S(2)}, u32[]{:S(2)}) collective-permute-start(bf16[256,128]{1,0:T(8,128)(2,1)S(1)} %get-tuple-element.25), channel_id=1, source_target_pairs={{0,128},{128,256},{256,384},{384,0},{1,129},{129,257},{257,385},{3... | collective-permute-start | bytes 196616 | tf_op jit(solution)/shard_map/sum_over_row/ppermute | solution.py:40
  156.4 4.0 %collective-permute-start.8 = (bf16[256,128]{1,0:T(8,128)(2,1)S(1)}, bf16[256,128]{1,0:T(8,128)(2,1)S(1)}, u32[]{:S(2)}, u32[]{:S(2)}) collective-permute-start(bf16[256,128]{1,0:T(8,128)(2,1)S(1)} %get-tuple-element.26), channel_id=1, source_target_pairs={{0,256},{128,384},{256,0},{384,128},{1,257},{129,385},{257,1},{385... | collective-permute-start | bytes 196616 | tf_op jit(solution)/shard_map/sum_over_row/ppermute | solution.py:40
  160.4 2.9 %collective-permute-start.9 = (bf16[256,128]{1,0:T(8,128)(2,1)S(1)}, bf16[256,128]{1,0:T(8,128)(2,1)S(1)}, u32[]{:S(2)}, u32[]{:S(2)}) collective-permute-start(bf16[256,128]{1,0:T(8,128)(2,1)S(1)} %get-tuple-element.27), channel_id=1, source_target_pairs={{0,384},{128,0},{256,128},{384,256},{1,385},{129,1},{257,129},{385... | collective-permute-start | bytes 196616 | tf_op jit(solution)/shard_map/sum_over_row/ppermute | solution.py:40
  163.3 0.0 collective-permute-done.7.near1
  163.3 0.8 collective-permute-done.8.near2
  164.1 2.5 %collective-permute-done.9.near3 = bf16[256,128]{1,0:T(8,128)(2,1)S(1)} collective-permute-done((bf16[256,128]{1,0:T(8,128)(2,1)S(1)}, bf16[256,128]{1,0:T(8,128)(2,1)S(1)}, u32[]{:S(2)}, u32[]{:S(2)}) %collective-permute-start.9) | collective-permute-done | bytes 65568 | tf_op jit(solution)/shard_map/sum_over_row/ppermute | solution.py:40
  166.5 1.0 all-to-all-done.7.parts
  167.6 0.8 last_sum.1
  168.4 16.0 %all_to_all.50 = bf16[16,16,256]{2,1,0:T(8,128)(2,1)S(1)} all-to-all(bf16[16,16,256]{2,1,0:T(8,128)(2,1)S(1)} %get-tuple-element.29), channel_id=1, replica_groups=mesh['y'=4,'zh'=4,'co'=2,'x'=4,'zl'=4] {'x','zl'}, dimensions={0} | all-to-all | bytes 262144 | tf_op jit(solution)/shard_map/gather_weight_grad/all_to_all | solution.py:27
  184.3 0.7 bitcast_convert_fusion
  (3 shorter events, 0.0 us)
Async XLA Ops:
  2.2 33.6 %all-to-all-start = ((bf16[4,128,256]{2,1,0:T(8,128)(2,1)}), bf16[4,128,256]{2,1,0:T(8,128)(2,1)S(1)}, u32[]{:S(2)}, u32[]{:S(2)}) async-start(bf16[4,128,256]{2,1,0:T(8,128)(2,1)} %broadcast_in_dim.4), calls=%async_computation | async-start | bytes 524288 | tf_op jit(solution)/shard_map/gather_features/all_to_all | solution.py:27
  17.3 35.4 %copy-start.3 = (s32[1,1,96,2]{2,3,1,0:T(2,128)S(1)}, s32[1,1,96,2]{2,3,1,0:T(2,128)}, u32[]{:S(2)}) copy-start(s32[1,1,96,2]{2,3,1,0:T(2,128)} %param.9) | copy-start | bytes 2308
  17.3 11.1 %collective-permute-start = (bf16[128,256]{1,0:T(8,128)(2,1)}, bf16[128,256]{1,0:T(8,128)(2,1)S(1)}, u32[]{:S(2)}, u32[]{:S(2)}) collective-permute-start(bf16[128,256]{1,0:T(8,128)(2,1)} %param.5), channel_id=1, source_target_pairs={{0,128},{128,256},{256,384},{384,0},{1,129},{129,257},{257,385},{3... | collective-permute-start | bytes 196616 | tf_op jit(solution)/shard_map/gather_features/ppermute | solution.py:40
  20.9 7.5 %collective-permute-start.2 = (bf16[128,256]{1,0:T(8,128)(2,1)}, bf16[128,256]{1,0:T(8,128)(2,1)S(1)}, u32[]{:S(2)}, u32[]{:S(2)}) collective-permute-start(bf16[128,256]{1,0:T(8,128)(2,1)} %param.5), channel_id=1, source_target_pairs={{0,384},{128,0},{256,128},{384,256},{1,385},{129,1},{257,129},{385... | collective-permute-start | bytes 196616 | tf_op jit(solution)/shard_map/gather_features/ppermute | solution.py:40
  24.5 7.9 %collective-permute-start.1 = (bf16[128,256]{1,0:T(8,128)(2,1)}, bf16[128,256]{1,0:T(8,128)(2,1)S(1)}, u32[]{:S(2)}, u32[]{:S(2)}) collective-permute-start(bf16[128,256]{1,0:T(8,128)(2,1)} %param.5), channel_id=1, source_target_pairs={{0,256},{128,384},{256,0},{384,128},{1,257},{129,385},{257,1},{385... | collective-permute-start | bytes 196616 | tf_op jit(solution)/shard_map/gather_features/ppermute | solution.py:40
  36.8 14.0 %all-to-all-start.1 = ((bf16[4,3,128,256]{3,2,1,0:T(8,128)(2,1)}), bf16[4,3,128,256]{3,2,1,0:T(8,128)(2,1)S(1)}, u32[]{:S(2)}, u32[]{:S(2)}) async-start(bf16[4,3,128,256]{3,2,1,0:T(8,128)(2,1)} %get-tuple-element.17), calls=%async_computation.1 | async-start | bytes 1572864 | tf_op jit(solution)/shard_map/gather_features/all_to_all | solution.py:27
  41.3 3.4 %collective-permute-start.3 = (bf16[4,128,256]{2,1,0:T(8,128)(2,1)S(1)}, bf16[4,128,256]{2,1,0:T(8,128)(2,1)S(1)}, u32[]{:S(2)}, u32[]{:S(2)}) collective-permute-start(bf16[4,128,256]{2,1,0:T(8,128)(2,1)S(1)} %get-tuple-element.16.near), channel_id=1, source_target_pairs={{0,16},{16,0},{1,17},{17,1},{2,18},{18,2},{3,19},{19,3},{4,20},{20... | collective-permute-start | bytes 786440 | tf_op jit(solution)/shard_map/gather_features/ppermute | solution.py:35
  50.7 4.2 %collective-permute-start.4 = (bf16[4,3,128,256]{3,2,1,0:T(8,128)(2,1)S(1)}, bf16[4,3,128,256]{3,2,1,0:T(8,128)(2,1)S(1)}, u32[]{:S(2)}, u32[]{:S(2)}) collective-permute-start(bf16[4,3,128,256]{3,2,1,0:T(8,128)(2,1)S(1)} %all-to-all-done.1.far), channel_id=1, source_target_pairs={{0,16},{16,0},{1,17},{17,1},{2,18},{18,2},{3,19},{19,3},{4,20},{20... | collective-permute-start | bytes 2359304 | tf_op jit(solution)/shard_map/gather_features/ppermute | solution.py:35
  76.9 14.0 %copy-start.1 = (bf16[256,256]{1,0:T(8,128)(2,1)S(1)}, bf16[256,256]{1,0:T(8,128)(2,1)}, u32[]{:S(2)}) copy-start(bf16[256,256]{1,0:T(8,128)(2,1)} %weight.3) | copy-start | bytes 393220
  76.9 14.0 %copy-start.2 = (bf16[128,256]{1,0:T(8,128)(2,1)S(1)}, bf16[128,256]{1,0:T(8,128)(2,1)}, u32[]{:S(2)}) copy-start(bf16[128,256]{1,0:T(8,128)(2,1)} %grad_out.1) | copy-start | bytes 196612
  103.0 16.8 %copy-start = (bf16[1,1,96,128,128]{4,3,2,1,0:T(8,128)(2,1)S(1)}, bf16[1,1,96,128,128]{4,3,2,1,0:T(8,128)(2,1)}, u32[]{:S(2)}) copy-start(bf16[1,1,96,128,128]{4,3,2,1,0:T(8,128)(2,1)} %param.8) | copy-start | bytes 9437188
  123.8 4.2 %collective-permute-start.5 = (bf16[3136,128]{1,0:T(8,128)(2,1)S(1)}, bf16[3136,128]{1,0:T(8,128)(2,1)S(1)}, u32[]{:S(2)}, u32[]{:S(2)}) collective-permute-start(bf16[3136,128]{1,0:T(8,128)(2,1)S(1)} %get-tuple-element.21), channel_id=1, source_target_pairs={{0,16},{16,0},{1,17},{17,1},{2,18},{18,2},{3,19},{19,3},{4,20},{20... | collective-permute-start | bytes 2408456 | tf_op jit(solution)/shard_map/sum_over_row/ppermute | solution.py:35
  145.0 22.6 %all-to-all-start.7 = ((bf16[4,288,128]{2,1,0:T(8,128)(2,1)}), bf16[4,288,128]{2,1,0:T(8,128)(2,1)S(1)}, u32[]{:S(2)}, u32[]{:S(2)}) async-start(bf16[4,288,128]{2,1,0:T(8,128)(2,1)} %y_sum.1), calls=%async_computation.7 | async-start | bytes 589824 | tf_op jit(solution)/shard_map/sum_over_row/all_to_all | solution.py:27
  150.4 3.4 %collective-permute-start.6 = (bf16[4,256,128]{2,1,0:T(8,128)(2,1)S(1)}, bf16[4,256,128]{2,1,0:T(8,128)(2,1)S(1)}, u32[]{:S(2)}, u32[]{:S(2)}) collective-permute-start(bf16[4,256,128]{2,1,0:T(8,128)(2,1)S(1)} %get-tuple-element.23), channel_id=1, source_target_pairs={{0,16},{16,0},{1,17},{17,1},{2,18},{18,2},{3,19},{19,3},{4,20},{20... | collective-permute-start | bytes 786440 | tf_op jit(solution)/shard_map/sum_over_row/ppermute | solution.py:35
  153.9 9.4 %collective-permute-start.7 = (bf16[256,128]{1,0:T(8,128)(2,1)S(1)}, bf16[256,128]{1,0:T(8,128)(2,1)S(1)}, u32[]{:S(2)}, u32[]{:S(2)}) collective-permute-start(bf16[256,128]{1,0:T(8,128)(2,1)S(1)} %get-tuple-element.25), channel_id=1, source_target_pairs={{0,128},{128,256},{256,384},{384,0},{1,129},{129,257},{257,385},{3... | collective-permute-start | bytes 196616 | tf_op jit(solution)/shard_map/sum_over_row/ppermute | solution.py:40
  156.4 7.7 %collective-permute-start.8 = (bf16[256,128]{1,0:T(8,128)(2,1)S(1)}, bf16[256,128]{1,0:T(8,128)(2,1)S(1)}, u32[]{:S(2)}, u32[]{:S(2)}) collective-permute-start(bf16[256,128]{1,0:T(8,128)(2,1)S(1)} %get-tuple-element.26), channel_id=1, source_target_pairs={{0,256},{128,384},{256,0},{384,128},{1,257},{129,385},{257,1},{385... | collective-permute-start | bytes 196616 | tf_op jit(solution)/shard_map/sum_over_row/ppermute | solution.py:40
  160.4 6.2 %collective-permute-start.9 = (bf16[256,128]{1,0:T(8,128)(2,1)S(1)}, bf16[256,128]{1,0:T(8,128)(2,1)S(1)}, u32[]{:S(2)}, u32[]{:S(2)}) collective-permute-start(bf16[256,128]{1,0:T(8,128)(2,1)S(1)} %get-tuple-element.27), channel_id=1, source_target_pairs={{0,384},{128,0},{256,128},{384,256},{1,385},{129,1},{257,129},{385... | collective-permute-start | bytes 196616 | tf_op jit(solution)/shard_map/sum_over_row/ppermute | solution.py:40

commit v4 on v3

--- a/solution.py
+++ b/solution.py
@@ -163,7 +163,7 @@
         return carry
 
     lax.fori_loop(0, tiles.shape[0] // GROUP, step, 0)
-    pair = split_pair(weight_grad)
+    pair = split_pair(weight_grad * (1.0 / math.sqrt(T * math.prod(SIZES.values()))))
     rows = FAR * H
     for first, near, far in ((0, mine_near, mine_far), (half, other_near, other_far)):
         for i in range(N):
@@ -217,8 +217,7 @@
         grad = grad + parts[s, H:].astype(F32)
     out[...] = total.T.astype(BF16)
     share = grad.shape[0] // 2
-    scale = 1.0 / math.sqrt(T * math.prod(SIZES.values()))
-    grad = jnp.concatenate([grad[:share], grad[share:]], axis=1) * scale
+    grad = jnp.concatenate([grad[:share], grad[share:]], axis=1)
     for c in range(NX * NZL):
         weight_grad[c] = grad.astype(BF16)
 

time: 187 us -> 187 us (level)
  no operation moved by 1% of the time
where the time goes in v4:
time: 187 us; the launch traced here: 185 us
  blocking collectives  91.9 us (49%)
  starting transfers between devices  53.1 us (28%)
  waiting for transfers between devices  25.1 us (13%)
  Pallas kernels  11.3 us (6%)
  local copies, waits for them, and re-layouts  2.05 us (1%)
    all_to_all x6, blocking collectives, exchange(): return lax.all_to_all(value, axis, 0, 0, tiled=True)  91.9 us
    all_to_all x3, starting transfers between devices, exchange(): return lax.all_to_all(value, axis, 0, 0, tiled=True)  25 us
    ppermute x6, starting transfers between devices, shift(): lax.ppermute(value, axis, [(i, (i + distance) % n) for i in range(n)])  20.4 us
    all_to_all x3, waiting for transfers between devices, exchange(): return lax.all_to_all(value, axis, 0, 0, tiled=True)  10.6 us
    ppermute x4, starting transfers between devices, swap_cores(): return lax.ppermute(value, 'co', [(0, 1), (1, 0)])  7.65 us
    ppermute x4, waiting for transfers between devices, swap_cores(): return lax.ppermute(value, 'co', [(0, 1), (1, 0)])  7.27 us
    ppermute x6, waiting for transfers between devices, shift(): lax.ppermute(value, axis, [(i, (i + distance) % n) for i in range(n)])  7.19 us
    pallas_call x1, Pallas kernels, on_device(): call(forward_kernel, [shape(row_tiles, T, H)], [SMEM] * 4 + [pltpu.HBM] +...  4.06 us
  transfers between devices with their start and end apart: 13, of which 10 were waited for; matrix products, arithmetic and copies ran while one was open for 0% of the time, Pallas kernels for 0%

profile of v4, /device:TPU:6, one launch (start us, length us, event | category | flops | bytes accessed | tf_op | source)
XLA Modules:
  0.0 185.1 jit_solution(13443485098351652460)
XLA Ops:
  0.6 1.6 broadcast_in_dim.4
  2.2 15.1 %all-to-all-start = ((bf16[4,128,256]{2,1,0:T(8,128)(2,1)}), bf16[4,128,256]{2,1,0:T(8,128)(2,1)S(1)}, u32[]{:S(2)}, u32[]{:S(2)}) async-start(bf16[4,128,256]{2,1,0:T(8,128)(2,1)} %broadcast_in_dim.4), calls=%async_computation | async-start | bytes 524288 | tf_op jit(solution)/shard_map/gather_features/all_to_all | solution.py:27
  17.3 0.0 copy-start.3
  17.3 3.6 %collective-permute-start = (bf16[128,256]{1,0:T(8,128)(2,1)}, bf16[128,256]{1,0:T(8,128)(2,1)S(1)}, u32[]{:S(2)}, u32[]{:S(2)}) collective-permute-start(bf16[128,256]{1,0:T(8,128)(2,1)} %param.5), channel_id=1, source_target_pairs={{0,128},{128,256},{256,384},{384,0},{1,129},{129,257},{257,385},{3... | collective-permute-start | bytes 196616 | tf_op jit(solution)/shard_map/gather_features/ppermute | solution.py:40
  20.9 3.6 %collective-permute-start.2 = (bf16[128,256]{1,0:T(8,128)(2,1)}, bf16[128,256]{1,0:T(8,128)(2,1)S(1)}, u32[]{:S(2)}, u32[]{:S(2)}) collective-permute-start(bf16[128,256]{1,0:T(8,128)(2,1)} %param.5), channel_id=1, source_target_pairs={{0,384},{128,0},{256,128},{384,256},{1,385},{129,1},{257,129},{385... | collective-permute-start | bytes 196616 | tf_op jit(solution)/shard_map/gather_features/ppermute | solution.py:40
  24.5 3.9 %collective-permute-start.1 = (bf16[128,256]{1,0:T(8,128)(2,1)}, bf16[128,256]{1,0:T(8,128)(2,1)S(1)}, u32[]{:S(2)}, u32[]{:S(2)}) collective-permute-start(bf16[128,256]{1,0:T(8,128)(2,1)} %param.5), channel_id=1, source_target_pairs={{0,256},{128,384},{256,0},{384,128},{1,257},{129,385},{257,1},{385... | collective-permute-start | bytes 196616 | tf_op jit(solution)/shard_map/gather_features/ppermute | solution.py:40
  28.4 0.0 collective-permute-done.near1
  28.4 0.0 collective-permute-done.2.near3
  28.4 3.9 %collective-permute-done.1.near2 = bf16[128,256]{1,0:T(8,128)(2,1)S(1)} collective-permute-done((bf16[128,256]{1,0:T(8,128)(2,1)}, bf16[128,256]{1,0:T(8,128)(2,1)S(1)}, u32[]{:S(2)}, u32[]{:S(2)}) %collective-permute-start.1) | collective-permute-done | bytes 65568 | tf_op jit(solution)/shard_map/gather_features/ppermute | solution.py:40
  32.3 3.5 %all-to-all-done.gathered = bf16[4,128,256]{2,1,0:T(8,128)(2,1)S(1)} async-done(((bf16[4,128,256]{2,1,0:T(8,128)(2,1)}), bf16[4,128,256]{2,1,0:T(8,128)(2,1)S(1)}, u32[]{:S(2)}, u32[]{:S(2)}) %all-to-all-start) | async-done | bytes 262176 | tf_op jit(solution)/shard_map/gather_features/all_to_all | solution.py:27
  35.8 1.0 far_copies.1
  36.8 4.5 %all-to-all-start.1 = ((bf16[4,3,128,256]{3,2,1,0:T(8,128)(2,1)}), bf16[4,3,128,256]{3,2,1,0:T(8,128)(2,1)S(1)}, u32[]{:S(2)}, u32[]{:S(2)}) async-start(bf16[4,3,128,256]{3,2,1,0:T(8,128)(2,1)} %get-tuple-element.17), calls=%async_computation.1 | async-start | bytes 1572864 | tf_op jit(solution)/shard_map/gather_features/all_to_all | solution.py:27
  41.3 1.9 %collective-permute-start.3 = (bf16[4,128,256]{2,1,0:T(8,128)(2,1)S(1)}, bf16[4,128,256]{2,1,0:T(8,128)(2,1)S(1)}, u32[]{:S(2)}, u32[]{:S(2)}) collective-permute-start(bf16[4,128,256]{2,1,0:T(8,128)(2,1)S(1)} %get-tuple-element.16.near), channel_id=1, source_target_pairs={{0,16},{16,0},{1,17},{17,1},{2,18},{18,2},{3,19},{19,3},{4,20},{20... | collective-permute-start | bytes 786440 | tf_op jit(solution)/shard_map/gather_features/ppermute | solution.py:35
  43.2 1.5 collective-permute-done.3.near_other
  44.7 6.1 %all-to-all-done.1.far = bf16[4,3,128,256]{3,2,1,0:T(8,128)(2,1)S(1)} async-done(((bf16[4,3,128,256]{3,2,1,0:T(8,128)(2,1)}), bf16[4,3,128,256]{3,2,1,0:T(8,128)(2,1)S(1)}, u32[]{:S(2)}, u32[]{:S(2)}) %all-to-all-start.1) | async-done | bytes 786464 | tf_op jit(solution)/shard_map/gather_features/all_to_all | solution.py:27
  50.7 1.9 %collective-permute-start.4 = (bf16[4,3,128,256]{3,2,1,0:T(8,128)(2,1)S(1)}, bf16[4,3,128,256]{3,2,1,0:T(8,128)(2,1)S(1)}, u32[]{:S(2)}, u32[]{:S(2)}) collective-permute-start(bf16[4,3,128,256]{3,2,1,0:T(8,128)(2,1)S(1)} %all-to-all-done.1.far), channel_id=1, source_target_pairs={{0,16},{16,0},{1,17},{17,1},{2,18},{18,2},{3,19},{19,3},{4,20},{20... | collective-permute-start | bytes 2359304 | tf_op jit(solution)/shard_map/gather_features/ppermute | solution.py:35
  52.7 0.0 copy-done.3
  52.7 0.1 copy.8
  52.8 0.1 reshape_squeeze.3.coords
  52.9 2.0 %collective-permute-done.4.far_other = bf16[4,3,128,256]{3,2,1,0:T(8,128)(2,1)S(1)} collective-permute-done((bf16[4,3,128,256]{3,2,1,0:T(8,128)(2,1)S(1)}, bf16[4,3,128,256]{3,2,1,0:T(8,128)(2,1)S(1)}, u32[]{:S(2)}, u32[]{:S(2)}) %collective-permute-start.4) | collective-permute-done | bytes 786464 | tf_op jit(solution)/shard_map/gather_features/ppermute | solution.py:35
  54.9 4.1 %forward_products.1 = bf16[16,128,256]{2,1,0:T(8,128)(2,1)S(1)} custom-call(s32[192]{0:T(256)S(1)} %reshape_squeeze.3.coords, s32[1]{0:T(128)} %bitcast.1.core, s32[1]{0:T(128)} %bitcast.2.y, s32[1]{0:T(128)} %bitcast.zh, bf16[96,128,128]{2,1,0:T(8,128)(2,1)} %bitcast.15, bf16[4,128,256]{2,1,0:T(8,128)(2,1)S(1)} %get-tuple-element.16.near, ...), custom_call_target="tpu_custom_call" | custom-call | flops 805306368 | bytes 4194304 | tf_op jit(solution)/shard_map/forward_products/pallas_call | solution.py:269
  59.0 17.9 %all_to_all.45.parts = bf16[4,4,128,256]{3,2,1,0:T(8,128)(2,1)S(1)} all-to-all(bf16[4,4,128,256]{3,2,1,0:T(8,128)(2,1)S(1)} %bitcast.18), channel_id=1, replica_groups=mesh['y'=4,'zh'=4,'co'=2,'x'=4,'zl'=4] {'x'}, dimensions={0} | all-to-all | bytes 2097152 | tf_op jit(solution)/shard_map/sum_over_col/all_to_all | solution.py:27
  76.9 0.0 copy-start.1
  76.9 0.0 copy-start.2
  76.9 0.1 x_sum.1
  77.0 13.8 %all_to_all.46.parts = bf16[4,128,256]{2,1,0:T(8,128)(2,1)S(1)} all-to-all(bf16[4,128,256]{2,1,0:T(8,128)(2,1)S(1)} %x_sum.1), channel_id=1, replica_groups=mesh['y'=4,'zh'=4,'co'=2,'x'=4,'zl'=4] {'zl'}, dimensions={0} | all-to-all | bytes 524288 | tf_op jit(solution)/shard_map/sum_over_col/all_to_all | solution.py:27
  90.9 0.0 copy-done.1
  90.9 0.0 copy-done.2
  90.9 0.3 dense.1
  91.2 11.6 %all_to_all.47 = bf16[4,320,128]{2,1,0:T(8,128)(2,1)S(1)} all-to-all(bf16[4,320,128]{2,1,0:T(8,128)(2,1)S(1)} %dense.1), channel_id=1, replica_groups=mesh['y'=4,'zh'=4,'co'=2,'x'=4,'zl'=4] {'zl'}, dimensions={0} | all-to-all | bytes 655360 | tf_op jit(solution)/shard_map/gather_gradients/all_to_all | solution.py:27
  102.8 0.2 broadcast_in_dim.5
  103.0 0.0 copy-start
  103.0 0.1 pad_maximum_fusion
  103.1 16.7 %all_to_all.48 = bf16[4,4,272,128]{3,2,1,0:T(8,128)(2,1)S(1)} all-to-all(bf16[4,4,272,128]{3,2,1,0:T(8,128)(2,1)S(1)} %pad_maximum_fusion), channel_id=1, replica_groups=mesh['y'=4,'zh'=4,'co'=2,'x'=4,'zl'=4] {'x'}, dimensions={0} | all-to-all | bytes 2228224 | tf_op jit(solution)/shard_map/gather_gradients/all_to_all | solution.py:27
  119.7 0.0 copy-done
  119.7 4.0 %backward_products.1 = (bf16[4,256,128]{2,1,0:T(8,128)(2,1)S(1)}, bf16[3136,128]{1,0:T(8,128)(2,1)S(1)}, bf16[4,256,128]{2,1,0:T(8,128)(2,1)S(1)}, bf16[3136,128]{1,0:T(8,128)(2,1)S(1)}) custom-call(s32[192]{0:T(256)S(1)} %reshape_squeeze.3.coords, s32[1]{0:T(128)} %bitcast.1.core, s32[1]{0:T(128)} %bitcast.2.y, s32[1]{0:T(128)} %bitcast.zh, ...), custom_call_target="tpu_custom_call" | custom-call | flops 805306368 | bytes 8519680 | tf_op jit(solution)/shard_map/backward_products/pallas_call | solution.py:302
  123.8 1.9 %collective-permute-start.5 = (bf16[3136,128]{1,0:T(8,128)(2,1)S(1)}, bf16[3136,128]{1,0:T(8,128)(2,1)S(1)}, u32[]{:S(2)}, u32[]{:S(2)}) collective-permute-start(bf16[3136,128]{1,0:T(8,128)(2,1)S(1)} %get-tuple-element.21), channel_id=1, source_target_pairs={{0,16},{16,0},{1,17},{17,1},{2,18},{18,2},{3,19},{19,3},{4,20},{20... | collective-permute-start | bytes 2408456 | tf_op jit(solution)/shard_map/sum_over_row/ppermute | solution.py:35
  125.7 2.3 %collective-permute-done.5.other = bf16[3136,128]{1,0:T(8,128)(2,1)S(1)} collective-permute-done((bf16[3136,128]{1,0:T(8,128)(2,1)S(1)}, bf16[3136,128]{1,0:T(8,128)(2,1)S(1)}, u32[]{:S(2)}, u32[]{:S(2)}) %collective-permute-start.5) | collective-permute-done | bytes 802848 | tf_op jit(solution)/shard_map/sum_over_row/ppermute | solution.py:35
  128.0 0.2 core_sum.1
  128.2 16.0 %all_to_all.49.parts = bf16[4,832,128]{2,1,0:T(8,128)(2,1)S(1)} all-to-all(bf16[4,832,128]{2,1,0:T(8,128)(2,1)S(1)} %core_sum.1), channel_id=1, replica_groups=mesh['y'=4,'zh'=4,'co'=2,'x'=4,'zl'=4] {'y'}, dimensions={0} | all-to-all | bytes 1703936 | tf_op jit(solution)/shard_map/sum_over_row/all_to_all | solution.py:27
  144.1 0.8 y_sum.1
  145.0 5.5 %all-to-all-start.7 = ((bf16[4,288,128]{2,1,0:T(8,128)(2,1)}), bf16[4,288,128]{2,1,0:T(8,128)(2,1)S(1)}, u32[]{:S(2)}, u32[]{:S(2)}) async-start(bf16[4,288,128]{2,1,0:T(8,128)(2,1)} %y_sum.1), calls=%async_computation.7 | async-start | bytes 589824 | tf_op jit(solution)/shard_map/sum_over_row/all_to_all | solution.py:27
  150.4 1.9 %collective-permute-start.6 = (bf16[4,256,128]{2,1,0:T(8,128)(2,1)S(1)}, bf16[4,256,128]{2,1,0:T(8,128)(2,1)S(1)}, u32[]{:S(2)}, u32[]{:S(2)}) collective-permute-start(bf16[4,256,128]{2,1,0:T(8,128)(2,1)S(1)} %get-tuple-element.23), channel_id=1, source_target_pairs={{0,16},{16,0},{1,17},{17,1},{2,18},{18,2},{3,19},{19,3},{4,20},{20... | collective-permute-start | bytes 786440 | tf_op jit(solution)/shard_map/sum_over_row/ppermute | solution.py:35
  152.3 1.5 collective-permute-done.6.other
  153.9 0.1 near_sum.1
  153.9 2.5 %collective-permute-start.7 = (bf16[256,128]{1,0:T(8,128)(2,1)S(1)}, bf16[256,128]{1,0:T(8,128)(2,1)S(1)}, u32[]{:S(2)}, u32[]{:S(2)}) collective-permute-start(bf16[256,128]{1,0:T(8,128)(2,1)S(1)} %get-tuple-element.25), channel_id=1, source_target_pairs={{0,128},{128,256},{256,384},{384,0},{1,129},{129,257},{257,385},{3... | collective-permute-start | bytes 196616 | tf_op jit(solution)/shard_map/sum_over_row/ppermute | solution.py:40
  156.4 4.0 %collective-permute-start.8 = (bf16[256,128]{1,0:T(8,128)(2,1)S(1)}, bf16[256,128]{1,0:T(8,128)(2,1)S(1)}, u32[]{:S(2)}, u32[]{:S(2)}) collective-permute-start(bf16[256,128]{1,0:T(8,128)(2,1)S(1)} %get-tuple-element.26), channel_id=1, source_target_pairs={{0,256},{128,384},{256,0},{384,128},{1,257},{129,385},{257,1},{385... | collective-permute-start | bytes 196616 | tf_op jit(solution)/shard_map/sum_over_row/ppermute | solution.py:40
  160.4 2.9 %collective-permute-start.9 = (bf16[256,128]{1,0:T(8,128)(2,1)S(1)}, bf16[256,128]{1,0:T(8,128)(2,1)S(1)}, u32[]{:S(2)}, u32[]{:S(2)}) collective-permute-start(bf16[256,128]{1,0:T(8,128)(2,1)S(1)} %get-tuple-element.27), channel_id=1, source_target_pairs={{0,384},{128,0},{256,128},{384,256},{1,385},{129,1},{257,129},{385... | collective-permute-start | bytes 196616 | tf_op jit(solution)/shard_map/sum_over_row/ppermute | solution.py:40
  163.3 0.0 collective-permute-done.7.near1
  163.3 0.8 collective-permute-done.8.near2
  164.1 2.5 %collective-permute-done.9.near3 = bf16[256,128]{1,0:T(8,128)(2,1)S(1)} collective-permute-done((bf16[256,128]{1,0:T(8,128)(2,1)S(1)}, bf16[256,128]{1,0:T(8,128)(2,1)S(1)}, u32[]{:S(2)}, u32[]{:S(2)}) %collective-permute-start.9) | collective-permute-done | bytes 65568 | tf_op jit(solution)/shard_map/sum_over_row/ppermute | solution.py:40
  166.5 1.0 all-to-all-done.7.parts
  167.6 0.8 last_sum.1
  168.4 16.0 %all_to_all.50 = bf16[16,16,256]{2,1,0:T(8,128)(2,1)S(1)} all-to-all(bf16[16,16,256]{2,1,0:T(8,128)(2,1)S(1)} %get-tuple-element.29), channel_id=1, replica_groups=mesh['y'=4,'zh'=4,'co'=2,'x'=4,'zl'=4] {'x','zl'}, dimensions={0} | all-to-all | bytes 262144 | tf_op jit(solution)/shard_map/gather_weight_grad/all_to_all | solution.py:27
  184.3 0.7 bitcast_convert_fusion
  (3 shorter events, 0.0 us)
Async XLA Ops:
  2.2 33.6 %all-to-all-start = ((bf16[4,128,256]{2,1,0:T(8,128)(2,1)}), bf16[4,128,256]{2,1,0:T(8,128)(2,1)S(1)}, u32[]{:S(2)}, u32[]{:S(2)}) async-start(bf16[4,128,256]{2,1,0:T(8,128)(2,1)} %broadcast_in_dim.4), calls=%async_computation | async-start | bytes 524288 | tf_op jit(solution)/shard_map/gather_features/all_to_all | solution.py:27
  17.3 35.4 %copy-start.3 = (s32[1,1,96,2]{2,3,1,0:T(2,128)S(1)}, s32[1,1,96,2]{2,3,1,0:T(2,128)}, u32[]{:S(2)}) copy-start(s32[1,1,96,2]{2,3,1,0:T(2,128)} %param.9) | copy-start | bytes 2308
  17.3 11.1 %collective-permute-start = (bf16[128,256]{1,0:T(8,128)(2,1)}, bf16[128,256]{1,0:T(8,128)(2,1)S(1)}, u32[]{:S(2)}, u32[]{:S(2)}) collective-permute-start(bf16[128,256]{1,0:T(8,128)(2,1)} %param.5), channel_id=1, source_target_pairs={{0,128},{128,256},{256,384},{384,0},{1,129},{129,257},{257,385},{3... | collective-permute-start | bytes 196616 | tf_op jit(solution)/shard_map/gather_features/ppermute | solution.py:40
  20.9 7.5 %collective-permute-start.2 = (bf16[128,256]{1,0:T(8,128)(2,1)}, bf16[128,256]{1,0:T(8,128)(2,1)S(1)}, u32[]{:S(2)}, u32[]{:S(2)}) collective-permute-start(bf16[128,256]{1,0:T(8,128)(2,1)} %param.5), channel_id=1, source_target_pairs={{0,384},{128,0},{256,128},{384,256},{1,385},{129,1},{257,129},{385... | collective-permute-start | bytes 196616 | tf_op jit(solution)/shard_map/gather_features/ppermute | solution.py:40
  24.5 7.9 %collective-permute-start.1 = (bf16[128,256]{1,0:T(8,128)(2,1)}, bf16[128,256]{1,0:T(8,128)(2,1)S(1)}, u32[]{:S(2)}, u32[]{:S(2)}) collective-permute-start(bf16[128,256]{1,0:T(8,128)(2,1)} %param.5), channel_id=1, source_target_pairs={{0,256},{128,384},{256,0},{384,128},{1,257},{129,385},{257,1},{385... | collective-permute-start | bytes 196616 | tf_op jit(solution)/shard_map/gather_features/ppermute | solution.py:40
  36.8 14.0 %all-to-all-start.1 = ((bf16[4,3,128,256]{3,2,1,0:T(8,128)(2,1)}), bf16[4,3,128,256]{3,2,1,0:T(8,128)(2,1)S(1)}, u32[]{:S(2)}, u32[]{:S(2)}) async-start(bf16[4,3,128,256]{3,2,1,0:T(8,128)(2,1)} %get-tuple-element.17), calls=%async_computation.1 | async-start | bytes 1572864 | tf_op jit(solution)/shard_map/gather_features/all_to_all | solution.py:27
  41.3 3.4 %collective-permute-start.3 = (bf16[4,128,256]{2,1,0:T(8,128)(2,1)S(1)}, bf16[4,128,256]{2,1,0:T(8,128)(2,1)S(1)}, u32[]{:S(2)}, u32[]{:S(2)}) collective-permute-start(bf16[4,128,256]{2,1,0:T(8,128)(2,1)S(1)} %get-tuple-element.16.near), channel_id=1, source_target_pairs={{0,16},{16,0},{1,17},{17,1},{2,18},{18,2},{3,19},{19,3},{4,20},{20... | collective-permute-start | bytes 786440 | tf_op jit(solution)/shard_map/gather_features/ppermute | solution.py:35
  50.7 4.2 %collective-permute-start.4 = (bf16[4,3,128,256]{3,2,1,0:T(8,128)(2,1)S(1)}, bf16[4,3,128,256]{3,2,1,0:T(8,128)(2,1)S(1)}, u32[]{:S(2)}, u32[]{:S(2)}) collective-permute-start(bf16[4,3,128,256]{3,2,1,0:T(8,128)(2,1)S(1)} %all-to-all-done.1.far), channel_id=1, source_target_pairs={{0,16},{16,0},{1,17},{17,1},{2,18},{18,2},{3,19},{19,3},{4,20},{20... | collective-permute-start | bytes 2359304 | tf_op jit(solution)/shard_map/gather_features/ppermute | solution.py:35
  76.9 14.0 %copy-start.1 = (bf16[256,256]{1,0:T(8,128)(2,1)S(1)}, bf16[256,256]{1,0:T(8,128)(2,1)}, u32[]{:S(2)}) copy-start(bf16[256,256]{1,0:T(8,128)(2,1)} %weight.3) | copy-start | bytes 393220
  76.9 14.0 %copy-start.2 = (bf16[128,256]{1,0:T(8,128)(2,1)S(1)}, bf16[128,256]{1,0:T(8,128)(2,1)}, u32[]{:S(2)}) copy-start(bf16[128,256]{1,0:T(8,128)(2,1)} %grad_out.1) | copy-start | bytes 196612
  103.0 16.8 %copy-start = (bf16[1,1,96,128,128]{4,3,2,1,0:T(8,128)(2,1)S(1)}, bf16[1,1,96,128,128]{4,3,2,1,0:T(8,128)(2,1)}, u32[]{:S(2)}) copy-start(bf16[1,1,96,128,128]{4,3,2,1,0:T(8,128)(2,1)} %param.8) | copy-start | bytes 9437188
  123.8 4.2 %collective-permute-start.5 = (bf16[3136,128]{1,0:T(8,128)(2,1)S(1)}, bf16[3136,128]{1,0:T(8,128)(2,1)S(1)}, u32[]{:S(2)}, u32[]{:S(2)}) collective-permute-start(bf16[3136,128]{1,0:T(8,128)(2,1)S(1)} %get-tuple-element.21), channel_id=1, source_target_pairs={{0,16},{16,0},{1,17},{17,1},{2,18},{18,2},{3,19},{19,3},{4,20},{20... | collective-permute-start | bytes 2408456 | tf_op jit(solution)/shard_map/sum_over_row/ppermute | solution.py:35
  145.0 22.6 %all-to-all-start.7 = ((bf16[4,288,128]{2,1,0:T(8,128)(2,1)}), bf16[4,288,128]{2,1,0:T(8,128)(2,1)S(1)}, u32[]{:S(2)}, u32[]{:S(2)}) async-start(bf16[4,288,128]{2,1,0:T(8,128)(2,1)} %y_sum.1), calls=%async_computation.7 | async-start | bytes 589824 | tf_op jit(solution)/shard_map/sum_over_row/all_to_all | solution.py:27
  150.4 3.4 %collective-permute-start.6 = (bf16[4,256,128]{2,1,0:T(8,128)(2,1)S(1)}, bf16[4,256,128]{2,1,0:T(8,128)(2,1)S(1)}, u32[]{:S(2)}, u32[]{:S(2)}) collective-permute-start(bf16[4,256,128]{2,1,0:T(8,128)(2,1)S(1)} %get-tuple-element.23), channel_id=1, source_target_pairs={{0,16},{16,0},{1,17},{17,1},{2,18},{18,2},{3,19},{19,3},{4,20},{20... | collective-permute-start | bytes 786440 | tf_op jit(solution)/shard_map/sum_over_row/ppermute | solution.py:35
  153.9 9.4 %collective-permute-start.7 = (bf16[256,128]{1,0:T(8,128)(2,1)S(1)}, bf16[256,128]{1,0:T(8,128)(2,1)S(1)}, u32[]{:S(2)}, u32[]{:S(2)}) collective-permute-start(bf16[256,128]{1,0:T(8,128)(2,1)S(1)} %get-tuple-element.25), channel_id=1, source_target_pairs={{0,128},{128,256},{256,384},{384,0},{1,129},{129,257},{257,385},{3... | collective-permute-start | bytes 196616 | tf_op jit(solution)/shard_map/sum_over_row/ppermute | solution.py:40
  156.4 7.7 %collective-permute-start.8 = (bf16[256,128]{1,0:T(8,128)(2,1)S(1)}, bf16[256,128]{1,0:T(8,128)(2,1)S(1)}, u32[]{:S(2)}, u32[]{:S(2)}) collective-permute-start(bf16[256,128]{1,0:T(8,128)(2,1)S(1)} %get-tuple-element.26), channel_id=1, source_target_pairs={{0,256},{128,384},{256,0},{384,128},{1,257},{129,385},{257,1},{385... | collective-permute-start | bytes 196616 | tf_op jit(solution)/shard_map/sum_over_row/ppermute | solution.py:40
  160.4 6.2 %collective-permute-start.9 = (bf16[256,128]{1,0:T(8,128)(2,1)S(1)}, bf16[256,128]{1,0:T(8,128)(2,1)S(1)}, u32[]{:S(2)}, u32[]{:S(2)}) collective-permute-start(bf16[256,128]{1,0:T(8,128)(2,1)S(1)} %get-tuple-element.27), channel_id=1, source_target_pairs={{0,384},{128,0},{256,128},{384,256},{1,385},{129,1},{257,129},{385... | collective-permute-start | bytes 196616 | tf_op jit(solution)/shard_map/sum_over_row/ppermute | solution.py:40

commit v5 on v4

--- a/solution.py
+++ b/solution.py
@@ -19,6 +19,7 @@
 T = 128
 H = 256
 GROUP = 32
+BACK_GROUP = 48
 VMEM_LIMIT = 20 * 1024 * 1024
 VMEM_MOST = 48 * 1024 * 1024
 
@@ -151,18 +152,18 @@
 
     def step(g, carry):
         products = []
-        for u in range(GROUP):
-            k = g * GROUP + u
+        for u in range(BACK_GROUP):
+            k = g * BACK_GROUP + u
             products.append(jnp.dot(source[coords[2 * k]], tiles[k], preferred_element_type=F32))
-        for u in range(GROUP):
-            j = coords[2 * (g * GROUP + u) + 1]
+        for u in range(BACK_GROUP):
+            j = coords[2 * (g * BACK_GROUP + u) + 1]
             ahead = ((j >> 1) - my_zh) & FAR
             ahead_y = jnp.where(ahead == 0, ((j >> 3) - my_y) & FAR, j >> 3)
             at = ((j & 1) ^ me) * half + place(ahead_y, ahead)
             total[at] += products[u]
         return carry
 
-    lax.fori_loop(0, tiles.shape[0] // GROUP, step, 0)
+    lax.fori_loop(0, tiles.shape[0] // BACK_GROUP, step, 0)
     pair = split_pair(weight_grad * (1.0 / math.sqrt(T * math.prod(SIZES.values()))))
     rows = FAR * H
     for first, near, far in ((0, mine_near, mine_far), (half, other_near, other_far)):

time: 187 us -> 186 us (level)
  no operation moved by 1% of the time
where the time goes in v5:
time: 186 us; the launch traced here: 185 us
  blocking collectives  91.9 us (49%)
  starting transfers between devices  53.1 us (29%)
  waiting for transfers between devices  25.1 us (13%)
  Pallas kernels  11.2 us (6%)
  local copies, waits for them, and re-layouts  2.05 us (1%)
    all_to_all x6, blocking collectives, exchange(): return lax.all_to_all(value, axis, 0, 0, tiled=True)  91.9 us
    all_to_all x3, starting transfers between devices, exchange(): return lax.all_to_all(value, axis, 0, 0, tiled=True)  25 us
    ppermute x6, starting transfers between devices, shift(): lax.ppermute(value, axis, [(i, (i + distance) % n) for i in range(n)])  20.4 us
    all_to_all x3, waiting for transfers between devices, exchange(): return lax.all_to_all(value, axis, 0, 0, tiled=True)  10.6 us
    ppermute x4, starting transfers between devices, swap_cores(): return lax.ppermute(value, 'co', [(0, 1), (1, 0)])  7.65 us
    ppermute x4, waiting for transfers between devices, swap_cores(): return lax.ppermute(value, 'co', [(0, 1), (1, 0)])  7.27 us
    ppermute x6, waiting for transfers between devices, shift(): lax.ppermute(value, axis, [(i, (i + distance) % n) for i in range(n)])  7.19 us
    pallas_call x1, Pallas kernels, on_device(): call(forward_kernel, [shape(row_tiles, T, H)], [SMEM] * 4 + [pltpu.HBM] +...  4.06 us
  transfers between devices with their start and end apart: 13, of which 10 were waited for; matrix products, arithmetic and copies ran while one was open for 0% of the time, Pallas kernels for 0%

profile of v5, /device:TPU:6, one launch (start us, length us, event | category | flops | bytes accessed | tf_op | source)
XLA Modules:
  0.0 184.9 jit_solution(16190615318949106366)
XLA Ops:
  0.6 1.6 broadcast_in_dim.4
  2.2 15.1 %all-to-all-start = ((bf16[4,128,256]{2,1,0:T(8,128)(2,1)}), bf16[4,128,256]{2,1,0:T(8,128)(2,1)S(1)}, u32[]{:S(2)}, u32[]{:S(2)}) async-start(bf16[4,128,256]{2,1,0:T(8,128)(2,1)} %broadcast_in_dim.4), calls=%async_computation | async-start | bytes 524288 | tf_op jit(solution)/shard_map/gather_features/all_to_all | solution.py:28
  17.3 0.0 copy-start.3
  17.3 3.6 %collective-permute-start = (bf16[128,256]{1,0:T(8,128)(2,1)}, bf16[128,256]{1,0:T(8,128)(2,1)S(1)}, u32[]{:S(2)}, u32[]{:S(2)}) collective-permute-start(bf16[128,256]{1,0:T(8,128)(2,1)} %param.5), channel_id=1, source_target_pairs={{0,128},{128,256},{256,384},{384,0},{1,129},{129,257},{257,385},{3... | collective-permute-start | bytes 196616 | tf_op jit(solution)/shard_map/gather_features/ppermute | solution.py:41
  20.9 3.6 %collective-permute-start.2 = (bf16[128,256]{1,0:T(8,128)(2,1)}, bf16[128,256]{1,0:T(8,128)(2,1)S(1)}, u32[]{:S(2)}, u32[]{:S(2)}) collective-permute-start(bf16[128,256]{1,0:T(8,128)(2,1)} %param.5), channel_id=1, source_target_pairs={{0,384},{128,0},{256,128},{384,256},{1,385},{129,1},{257,129},{385... | collective-permute-start | bytes 196616 | tf_op jit(solution)/shard_map/gather_features/ppermute | solution.py:41
  24.5 3.9 %collective-permute-start.1 = (bf16[128,256]{1,0:T(8,128)(2,1)}, bf16[128,256]{1,0:T(8,128)(2,1)S(1)}, u32[]{:S(2)}, u32[]{:S(2)}) collective-permute-start(bf16[128,256]{1,0:T(8,128)(2,1)} %param.5), channel_id=1, source_target_pairs={{0,256},{128,384},{256,0},{384,128},{1,257},{129,385},{257,1},{385... | collective-permute-start | bytes 196616 | tf_op jit(solution)/shard_map/gather_features/ppermute | solution.py:41
  28.4 0.0 collective-permute-done.near1
  28.4 0.0 collective-permute-done.2.near3
  28.4 3.9 %collective-permute-done.1.near2 = bf16[128,256]{1,0:T(8,128)(2,1)S(1)} collective-permute-done((bf16[128,256]{1,0:T(8,128)(2,1)}, bf16[128,256]{1,0:T(8,128)(2,1)S(1)}, u32[]{:S(2)}, u32[]{:S(2)}) %collective-permute-start.1) | collective-permute-done | bytes 65568 | tf_op jit(solution)/shard_map/gather_features/ppermute | solution.py:41
  32.3 3.5 %all-to-all-done.gathered = bf16[4,128,256]{2,1,0:T(8,128)(2,1)S(1)} async-done(((bf16[4,128,256]{2,1,0:T(8,128)(2,1)}), bf16[4,128,256]{2,1,0:T(8,128)(2,1)S(1)}, u32[]{:S(2)}, u32[]{:S(2)}) %all-to-all-start) | async-done | bytes 262176 | tf_op jit(solution)/shard_map/gather_features/all_to_all | solution.py:28
  35.8 1.0 far_copies.1
  36.8 4.5 %all-to-all-start.1 = ((bf16[4,3,128,256]{3,2,1,0:T(8,128)(2,1)}), bf16[4,3,128,256]{3,2,1,0:T(8,128)(2,1)S(1)}, u32[]{:S(2)}, u32[]{:S(2)}) async-start(bf16[4,3,128,256]{3,2,1,0:T(8,128)(2,1)} %get-tuple-element.17), calls=%async_computation.1 | async-start | bytes 1572864 | tf_op jit(solution)/shard_map/gather_features/all_to_all | solution.py:28
  41.3 1.9 %collective-permute-start.3 = (bf16[4,128,256]{2,1,0:T(8,128)(2,1)S(1)}, bf16[4,128,256]{2,1,0:T(8,128)(2,1)S(1)}, u32[]{:S(2)}, u32[]{:S(2)}) collective-permute-start(bf16[4,128,256]{2,1,0:T(8,128)(2,1)S(1)} %get-tuple-element.16.near), channel_id=1, source_target_pairs={{0,16},{16,0},{1,17},{17,1},{2,18},{18,2},{3,19},{19,3},{4,20},{20... | collective-permute-start | bytes 786440 | tf_op jit(solution)/shard_map/gather_features/ppermute | solution.py:36
  43.2 1.5 collective-permute-done.3.near_other
  44.7 6.1 %all-to-all-done.1.far = bf16[4,3,128,256]{3,2,1,0:T(8,128)(2,1)S(1)} async-done(((bf16[4,3,128,256]{3,2,1,0:T(8,128)(2,1)}), bf16[4,3,128,256]{3,2,1,0:T(8,128)(2,1)S(1)}, u32[]{:S(2)}, u32[]{:S(2)}) %all-to-all-start.1) | async-done | bytes 786464 | tf_op jit(solution)/shard_map/gather_features/all_to_all | solution.py:28
  50.7 1.9 %collective-permute-start.4 = (bf16[4,3,128,256]{3,2,1,0:T(8,128)(2,1)S(1)}, bf16[4,3,128,256]{3,2,1,0:T(8,128)(2,1)S(1)}, u32[]{:S(2)}, u32[]{:S(2)}) collective-permute-start(bf16[4,3,128,256]{3,2,1,0:T(8,128)(2,1)S(1)} %all-to-all-done.1.far), channel_id=1, source_target_pairs={{0,16},{16,0},{1,17},{17,1},{2,18},{18,2},{3,19},{19,3},{4,20},{20... | collective-permute-start | bytes 2359304 | tf_op jit(solution)/shard_map/gather_features/ppermute | solution.py:36
  52.7 0.0 copy-done.3
  52.7 0.1 copy.8
  52.8 0.1 reshape_squeeze.3.coords
  52.9 2.0 %collective-permute-done.4.far_other = bf16[4,3,128,256]{3,2,1,0:T(8,128)(2,1)S(1)} collective-permute-done((bf16[4,3,128,256]{3,2,1,0:T(8,128)(2,1)S(1)}, bf16[4,3,128,256]{3,2,1,0:T(8,128)(2,1)S(1)}, u32[]{:S(2)}, u32[]{:S(2)}) %collective-permute-start.4) | collective-permute-done | bytes 786464 | tf_op jit(solution)/shard_map/gather_features/ppermute | solution.py:36
  54.9 4.1 %forward_products.1 = bf16[16,128,256]{2,1,0:T(8,128)(2,1)S(1)} custom-call(s32[192]{0:T(256)S(1)} %reshape_squeeze.3.coords, s32[1]{0:T(128)} %bitcast.1.core, s32[1]{0:T(128)} %bitcast.2.y, s32[1]{0:T(128)} %bitcast.zh, bf16[96,128,128]{2,1,0:T(8,128)(2,1)} %bitcast.15, bf16[4,128,256]{2,1,0:T(8,128)(2,1)S(1)} %get-tuple-element.16.near, ...), custom_call_target="tpu_custom_call" | custom-call | flops 805306368 | bytes 4194304 | tf_op jit(solution)/shard_map/forward_products/pallas_call | solution.py:270
  59.0 17.9 %all_to_all.45.parts = bf16[4,4,128,256]{3,2,1,0:T(8,128)(2,1)S(1)} all-to-all(bf16[4,4,128,256]{3,2,1,0:T(8,128)(2,1)S(1)} %bitcast.18), channel_id=1, replica_groups=mesh['y'=4,'zh'=4,'co'=2,'x'=4,'zl'=4] {'x'}, dimensions={0} | all-to-all | bytes 2097152 | tf_op jit(solution)/shard_map/sum_over_col/all_to_all | solution.py:28
  76.9 0.0 copy-start.1
  76.9 0.0 copy-start.2
  76.9 0.1 x_sum.1
  77.0 13.8 %all_to_all.46.parts = bf16[4,128,256]{2,1,0:T(8,128)(2,1)S(1)} all-to-all(bf16[4,128,256]{2,1,0:T(8,128)(2,1)S(1)} %x_sum.1), channel_id=1, replica_groups=mesh['y'=4,'zh'=4,'co'=2,'x'=4,'zl'=4] {'zl'}, dimensions={0} | all-to-all | bytes 524288 | tf_op jit(solution)/shard_map/sum_over_col/all_to_all | solution.py:28
  90.9 0.0 copy-done.1
  90.9 0.0 copy-done.2
  90.9 0.3 dense.1
  91.2 11.6 %all_to_all.47 = bf16[4,320,128]{2,1,0:T(8,128)(2,1)S(1)} all-to-all(bf16[4,320,128]{2,1,0:T(8,128)(2,1)S(1)} %dense.1), channel_id=1, replica_groups=mesh['y'=4,'zh'=4,'co'=2,'x'=4,'zl'=4] {'zl'}, dimensions={0} | all-to-all | bytes 655360 | tf_op jit(solution)/shard_map/gather_gradients/all_to_all | solution.py:28
  102.8 0.2 broadcast_in_dim.5
  103.0 0.0 copy-start
  103.0 0.1 pad_maximum_fusion
  103.1 16.7 %all_to_all.48 = bf16[4,4,272,128]{3,2,1,0:T(8,128)(2,1)S(1)} all-to-all(bf16[4,4,272,128]{3,2,1,0:T(8,128)(2,1)S(1)} %pad_maximum_fusion), channel_id=1, replica_groups=mesh['y'=4,'zh'=4,'co'=2,'x'=4,'zl'=4] {'x'}, dimensions={0} | all-to-all | bytes 2228224 | tf_op jit(solution)/shard_map/gather_gradients/all_to_all | solution.py:28
  119.7 0.0 copy-done
  119.7 3.9 %backward_products.1 = (bf16[4,256,128]{2,1,0:T(8,128)(2,1)S(1)}, bf16[3136,128]{1,0:T(8,128)(2,1)S(1)}, bf16[4,256,128]{2,1,0:T(8,128)(2,1)S(1)}, bf16[3136,128]{1,0:T(8,128)(2,1)S(1)}) custom-call(s32[192]{0:T(256)S(1)} %reshape_squeeze.3.coords, s32[1]{0:T(128)} %bitcast.1.core, s32[1]{0:T(128)} %bitcast.2.y, s32[1]{0:T(128)} %bitcast.zh, ...), custom_call_target="tpu_custom_call" | custom-call | flops 805306368 | bytes 8519680 | tf_op jit(solution)/shard_map/backward_products/pallas_call | solution.py:303
  123.6 1.9 %collective-permute-start.5 = (bf16[3136,128]{1,0:T(8,128)(2,1)S(1)}, bf16[3136,128]{1,0:T(8,128)(2,1)S(1)}, u32[]{:S(2)}, u32[]{:S(2)}) collective-permute-start(bf16[3136,128]{1,0:T(8,128)(2,1)S(1)} %get-tuple-element.21), channel_id=1, source_target_pairs={{0,16},{16,0},{1,17},{17,1},{2,18},{18,2},{3,19},{19,3},{4,20},{20... | collective-permute-start | bytes 2408456 | tf_op jit(solution)/shard_map/sum_over_row/ppermute | solution.py:36
  125.6 2.3 %collective-permute-done.5.other = bf16[3136,128]{1,0:T(8,128)(2,1)S(1)} collective-permute-done((bf16[3136,128]{1,0:T(8,128)(2,1)S(1)}, bf16[3136,128]{1,0:T(8,128)(2,1)S(1)}, u32[]{:S(2)}, u32[]{:S(2)}) %collective-permute-start.5) | collective-permute-done | bytes 802848 | tf_op jit(solution)/shard_map/sum_over_row/ppermute | solution.py:36
  127.9 0.2 core_sum.1
  128.0 16.0 %all_to_all.49.parts = bf16[4,832,128]{2,1,0:T(8,128)(2,1)S(1)} all-to-all(bf16[4,832,128]{2,1,0:T(8,128)(2,1)S(1)} %core_sum.1), channel_id=1, replica_groups=mesh['y'=4,'zh'=4,'co'=2,'x'=4,'zl'=4] {'y'}, dimensions={0} | all-to-all | bytes 1703936 | tf_op jit(solution)/shard_map/sum_over_row/all_to_all | solution.py:28
  144.0 0.8 y_sum.1
  144.8 5.5 %all-to-all-start.7 = ((bf16[4,288,128]{2,1,0:T(8,128)(2,1)}), bf16[4,288,128]{2,1,0:T(8,128)(2,1)S(1)}, u32[]{:S(2)}, u32[]{:S(2)}) async-start(bf16[4,288,128]{2,1,0:T(8,128)(2,1)} %y_sum.1), calls=%async_computation.7 | async-start | bytes 589824 | tf_op jit(solution)/shard_map/sum_over_row/all_to_all | solution.py:28
  150.3 1.9 %collective-permute-start.6 = (bf16[4,256,128]{2,1,0:T(8,128)(2,1)S(1)}, bf16[4,256,128]{2,1,0:T(8,128)(2,1)S(1)}, u32[]{:S(2)}, u32[]{:S(2)}) collective-permute-start(bf16[4,256,128]{2,1,0:T(8,128)(2,1)S(1)} %get-tuple-element.23), channel_id=1, source_target_pairs={{0,16},{16,0},{1,17},{17,1},{2,18},{18,2},{3,19},{19,3},{4,20},{20... | collective-permute-start | bytes 786440 | tf_op jit(solution)/shard_map/sum_over_row/ppermute | solution.py:36
  152.2 1.5 collective-permute-done.6.other
  153.7 0.1 near_sum.1
  153.8 2.5 %collective-permute-start.7 = (bf16[256,128]{1,0:T(8,128)(2,1)S(1)}, bf16[256,128]{1,0:T(8,128)(2,1)S(1)}, u32[]{:S(2)}, u32[]{:S(2)}) collective-permute-start(bf16[256,128]{1,0:T(8,128)(2,1)S(1)} %get-tuple-element.25), channel_id=1, source_target_pairs={{0,128},{128,256},{256,384},{384,0},{1,129},{129,257},{257,385},{3... | collective-permute-start | bytes 196616 | tf_op jit(solution)/shard_map/sum_over_row/ppermute | solution.py:41
  156.3 4.0 %collective-permute-start.8 = (bf16[256,128]{1,0:T(8,128)(2,1)S(1)}, bf16[256,128]{1,0:T(8,128)(2,1)S(1)}, u32[]{:S(2)}, u32[]{:S(2)}) collective-permute-start(bf16[256,128]{1,0:T(8,128)(2,1)S(1)} %get-tuple-element.26), channel_id=1, source_target_pairs={{0,256},{128,384},{256,0},{384,128},{1,257},{129,385},{257,1},{385... | collective-permute-start | bytes 196616 | tf_op jit(solution)/shard_map/sum_over_row/ppermute | solution.py:41
  160.3 2.9 %collective-permute-start.9 = (bf16[256,128]{1,0:T(8,128)(2,1)S(1)}, bf16[256,128]{1,0:T(8,128)(2,1)S(1)}, u32[]{:S(2)}, u32[]{:S(2)}) collective-permute-start(bf16[256,128]{1,0:T(8,128)(2,1)S(1)} %get-tuple-element.27), channel_id=1, source_target_pairs={{0,384},{128,0},{256,128},{384,256},{1,385},{129,1},{257,129},{385... | collective-permute-start | bytes 196616 | tf_op jit(solution)/shard_map/sum_over_row/ppermute | solution.py:41
  163.2 0.0 collective-permute-done.7.near1
  163.2 0.8 collective-permute-done.8.near2
  163.9 2.5 %collective-permute-done.9.near3 = bf16[256,128]{1,0:T(8,128)(2,1)S(1)} collective-permute-done((bf16[256,128]{1,0:T(8,128)(2,1)S(1)}, bf16[256,128]{1,0:T(8,128)(2,1)S(1)}, u32[]{:S(2)}, u32[]{:S(2)}) %collective-permute-start.9) | collective-permute-done | bytes 65568 | tf_op jit(solution)/shard_map/sum_over_row/ppermute | solution.py:41
  166.4 1.0 all-to-all-done.7.parts
  167.5 0.8 last_sum.1
  168.2 16.0 %all_to_all.50 = bf16[16,16,256]{2,1,0:T(8,128)(2,1)S(1)} all-to-all(bf16[16,16,256]{2,1,0:T(8,128)(2,1)S(1)} %get-tuple-element.29), channel_id=1, replica_groups=mesh['y'=4,'zh'=4,'co'=2,'x'=4,'zl'=4] {'x','zl'}, dimensions={0} | all-to-all | bytes 262144 | tf_op jit(solution)/shard_map/gather_weight_grad/all_to_all | solution.py:28
  184.2 0.7 bitcast_convert_fusion
  (3 shorter events, 0.0 us)
Async XLA Ops:
  2.2 33.6 %all-to-all-start = ((bf16[4,128,256]{2,1,0:T(8,128)(2,1)}), bf16[4,128,256]{2,1,0:T(8,128)(2,1)S(1)}, u32[]{:S(2)}, u32[]{:S(2)}) async-start(bf16[4,128,256]{2,1,0:T(8,128)(2,1)} %broadcast_in_dim.4), calls=%async_computation | async-start | bytes 524288 | tf_op jit(solution)/shard_map/gather_features/all_to_all | solution.py:28
  17.3 35.4 %copy-start.3 = (s32[1,1,96,2]{2,3,1,0:T(2,128)S(1)}, s32[1,1,96,2]{2,3,1,0:T(2,128)}, u32[]{:S(2)}) copy-start(s32[1,1,96,2]{2,3,1,0:T(2,128)} %param.9) | copy-start | bytes 2308
  17.3 11.1 %collective-permute-start = (bf16[128,256]{1,0:T(8,128)(2,1)}, bf16[128,256]{1,0:T(8,128)(2,1)S(1)}, u32[]{:S(2)}, u32[]{:S(2)}) collective-permute-start(bf16[128,256]{1,0:T(8,128)(2,1)} %param.5), channel_id=1, source_target_pairs={{0,128},{128,256},{256,384},{384,0},{1,129},{129,257},{257,385},{3... | collective-permute-start | bytes 196616 | tf_op jit(solution)/shard_map/gather_features/ppermute | solution.py:41
  20.9 7.5 %collective-permute-start.2 = (bf16[128,256]{1,0:T(8,128)(2,1)}, bf16[128,256]{1,0:T(8,128)(2,1)S(1)}, u32[]{:S(2)}, u32[]{:S(2)}) collective-permute-start(bf16[128,256]{1,0:T(8,128)(2,1)} %param.5), channel_id=1, source_target_pairs={{0,384},{128,0},{256,128},{384,256},{1,385},{129,1},{257,129},{385... | collective-permute-start | bytes 196616 | tf_op jit(solution)/shard_map/gather_features/ppermute | solution.py:41
  24.5 7.9 %collective-permute-start.1 = (bf16[128,256]{1,0:T(8,128)(2,1)}, bf16[128,256]{1,0:T(8,128)(2,1)S(1)}, u32[]{:S(2)}, u32[]{:S(2)}) collective-permute-start(bf16[128,256]{1,0:T(8,128)(2,1)} %param.5), channel_id=1, source_target_pairs={{0,256},{128,384},{256,0},{384,128},{1,257},{129,385},{257,1},{385... | collective-permute-start | bytes 196616 | tf_op jit(solution)/shard_map/gather_features/ppermute | solution.py:41
  36.8 14.0 %all-to-all-start.1 = ((bf16[4,3,128,256]{3,2,1,0:T(8,128)(2,1)}), bf16[4,3,128,256]{3,2,1,0:T(8,128)(2,1)S(1)}, u32[]{:S(2)}, u32[]{:S(2)}) async-start(bf16[4,3,128,256]{3,2,1,0:T(8,128)(2,1)} %get-tuple-element.17), calls=%async_computation.1 | async-start | bytes 1572864 | tf_op jit(solution)/shard_map/gather_features/all_to_all | solution.py:28
  41.3 3.4 %collective-permute-start.3 = (bf16[4,128,256]{2,1,0:T(8,128)(2,1)S(1)}, bf16[4,128,256]{2,1,0:T(8,128)(2,1)S(1)}, u32[]{:S(2)}, u32[]{:S(2)}) collective-permute-start(bf16[4,128,256]{2,1,0:T(8,128)(2,1)S(1)} %get-tuple-element.16.near), channel_id=1, source_target_pairs={{0,16},{16,0},{1,17},{17,1},{2,18},{18,2},{3,19},{19,3},{4,20},{20... | collective-permute-start | bytes 786440 | tf_op jit(solution)/shard_map/gather_features/ppermute | solution.py:36
  50.7 4.2 %collective-permute-start.4 = (bf16[4,3,128,256]{3,2,1,0:T(8,128)(2,1)S(1)}, bf16[4,3,128,256]{3,2,1,0:T(8,128)(2,1)S(1)}, u32[]{:S(2)}, u32[]{:S(2)}) collective-permute-start(bf16[4,3,128,256]{3,2,1,0:T(8,128)(2,1)S(1)} %all-to-all-done.1.far), channel_id=1, source_target_pairs={{0,16},{16,0},{1,17},{17,1},{2,18},{18,2},{3,19},{19,3},{4,20},{20... | collective-permute-start | bytes 2359304 | tf_op jit(solution)/shard_map/gather_features/ppermute | solution.py:36
  76.9 14.0 %copy-start.1 = (bf16[256,256]{1,0:T(8,128)(2,1)S(1)}, bf16[256,256]{1,0:T(8,128)(2,1)}, u32[]{:S(2)}) copy-start(bf16[256,256]{1,0:T(8,128)(2,1)} %weight.3) | copy-start | bytes 393220
  76.9 14.0 %copy-start.2 = (bf16[128,256]{1,0:T(8,128)(2,1)S(1)}, bf16[128,256]{1,0:T(8,128)(2,1)}, u32[]{:S(2)}) copy-start(bf16[128,256]{1,0:T(8,128)(2,1)} %grad_out.1) | copy-start | bytes 196612
  103.0 16.8 %copy-start = (bf16[1,1,96,128,128]{4,3,2,1,0:T(8,128)(2,1)S(1)}, bf16[1,1,96,128,128]{4,3,2,1,0:T(8,128)(2,1)}, u32[]{:S(2)}) copy-start(bf16[1,1,96,128,128]{4,3,2,1,0:T(8,128)(2,1)} %param.8) | copy-start | bytes 9437188
  123.6 4.2 %collective-permute-start.5 = (bf16[3136,128]{1,0:T(8,128)(2,1)S(1)}, bf16[3136,128]{1,0:T(8,128)(2,1)S(1)}, u32[]{:S(2)}, u32[]{:S(2)}) collective-permute-start(bf16[3136,128]{1,0:T(8,128)(2,1)S(1)} %get-tuple-element.21), channel_id=1, source_target_pairs={{0,16},{16,0},{1,17},{17,1},{2,18},{18,2},{3,19},{19,3},{4,20},{20... | collective-permute-start | bytes 2408456 | tf_op jit(solution)/shard_map/sum_over_row/ppermute | solution.py:36
  144.8 22.6 %all-to-all-start.7 = ((bf16[4,288,128]{2,1,0:T(8,128)(2,1)}), bf16[4,288,128]{2,1,0:T(8,128)(2,1)S(1)}, u32[]{:S(2)}, u32[]{:S(2)}) async-start(bf16[4,288,128]{2,1,0:T(8,128)(2,1)} %y_sum.1), calls=%async_computation.7 | async-start | bytes 589824 | tf_op jit(solution)/shard_map/sum_over_row/all_to_all | solution.py:28
  150.3 3.4 %collective-permute-start.6 = (bf16[4,256,128]{2,1,0:T(8,128)(2,1)S(1)}, bf16[4,256,128]{2,1,0:T(8,128)(2,1)S(1)}, u32[]{:S(2)}, u32[]{:S(2)}) collective-permute-start(bf16[4,256,128]{2,1,0:T(8,128)(2,1)S(1)} %get-tuple-element.23), channel_id=1, source_target_pairs={{0,16},{16,0},{1,17},{17,1},{2,18},{18,2},{3,19},{19,3},{4,20},{20... | collective-permute-start | bytes 786440 | tf_op jit(solution)/shard_map/sum_over_row/ppermute | solution.py:36
  153.8 9.4 %collective-permute-start.7 = (bf16[256,128]{1,0:T(8,128)(2,1)S(1)}, bf16[256,128]{1,0:T(8,128)(2,1)S(1)}, u32[]{:S(2)}, u32[]{:S(2)}) collective-permute-start(bf16[256,128]{1,0:T(8,128)(2,1)S(1)} %get-tuple-element.25), channel_id=1, source_target_pairs={{0,128},{128,256},{256,384},{384,0},{1,129},{129,257},{257,385},{3... | collective-permute-start | bytes 196616 | tf_op jit(solution)/shard_map/sum_over_row/ppermute | solution.py:41
  156.3 7.7 %collective-permute-start.8 = (bf16[256,128]{1,0:T(8,128)(2,1)S(1)}, bf16[256,128]{1,0:T(8,128)(2,1)S(1)}, u32[]{:S(2)}, u32[]{:S(2)}) collective-permute-start(bf16[256,128]{1,0:T(8,128)(2,1)S(1)} %get-tuple-element.26), channel_id=1, source_target_pairs={{0,256},{128,384},{256,0},{384,128},{1,257},{129,385},{257,1},{385... | collective-permute-start | bytes 196616 | tf_op jit(solution)/shard_map/sum_over_row/ppermute | solution.py:41
  160.3 6.2 %collective-permute-start.9 = (bf16[256,128]{1,0:T(8,128)(2,1)S(1)}, bf16[256,128]{1,0:T(8,128)(2,1)S(1)}, u32[]{:S(2)}, u32[]{:S(2)}) collective-permute-start(bf16[256,128]{1,0:T(8,128)(2,1)S(1)} %get-tuple-element.27), channel_id=1, source_target_pairs={{0,384},{128,0},{256,128},{384,256},{1,385},{129,1},{257,129},{385... | collective-permute-start | bytes 196616 | tf_op jit(solution)/shard_map/sum_over_row/ppermute | solution.py:41
